TPU v7x, 512 devices: a whole 4x4x16 slice. The times are simulated.
512 devices in a mesh: seq: 64 (over y_hi, z, core), dp: 8 (over y_lo, x).
Axes of the slice: x: 4, y: 4 (y_hi: 2, y_lo: 2; y = y_hi * 2 + y_lo), z: 16, core: 2. Of those that a mesh axis runs over, the one named last changes fastest.
Arguments:
- queries: bfloat16 [65536, 768], P(('dp', 'seq')), parts along dimension 0, may hold values from -6.5 to 6.5, as said below
- key_states: bfloat16 [65536, 768], P(('dp', 'seq')), parts along dimension 0, may hold values from -6.5 to 6.5, as said below
- value_states: bfloat16 [65536, 768], P(('dp', 'seq')), parts along dimension 0, may hold values from -6 to 6
- grad_output: bfloat16 [65536, 768], P(('dp', 'seq')), parts along dimension 0, may hold values from -6 to 6
- head_offsets: int32 [4, 12], replicated, may hold values from 0 to 63, as said below
Outputs:
- attended: bfloat16 [65536, 768], P(('dp', 'seq')), parts along dimension 0
- grad_queries: bfloat16 [65536, 768], P(('dp', 'seq')), parts along dimension 0
- grad_keys: bfloat16 [65536, 768], P(('dp', 'seq')), parts along dimension 0
- grad_values: bfloat16 [65536, 768], P(('dp', 'seq')), parts along dimension 0
There are 8 independent parts, one for each index of `dp`. A program takes and returns all parts, laid end to end along the dimension named above; an argument that names none is the same for every part. Nothing has to cross between parts.
Inputs may be any that keep to these rules, and one draw needn't show every extreme that they name: `queries`: float entries, hot rows included. `key_states`: float entries, hot rows included. head_offsets[l, h] lies in 0 to g - 1 for level l's group size g (1, 4, 16, 64); at every level some head takes g - 1.
All inputs are finite; a program needn't handle non-finite values.
Results may differ from a plain program's by a relative error of at most 0.025.
Values may be sent and summed in bfloat16 or wider, within the bound.
No kernel may reach another device: no remote copies, remote signals or barrier semaphores. Data moves between devices by JAX's collectives and lax.ppermute only.
A program may use at most 64 MiB of HBM per device.

v0:
```python
import jax
import jax.numpy as jnp
from jax import lax
from jax.sharding import PartitionSpec as P

NEG_FILL = -1e30


def swapped(value, axis, stride):
    return lax.ppermute(value, axis, [(i, i ^ 1 << stride) for i in range(lax.axis_size(axis))])


def pick_rows(source, group, offset_row):
    rows, heads, width = source.shape
    shaped = source.reshape(rows // group, group, heads, width)
    onehot = jnp.arange(group, dtype=jnp.int32)[:, None] == offset_row[None, :]
    return jnp.sum(jnp.where(onehot[None, :, :, None], shaped, jnp.zeros((), source.dtype)), axis=1)


def place_rows(picked, group, offset_row, fill):
    rows, heads, width = picked.shape
    onehot = jnp.arange(group, dtype=jnp.int32)[:, None] == offset_row[None, :]
    spread = jnp.where(
        onehot[None, :, :, None], picked[:, None, :, :], jnp.asarray(fill, picked.dtype)
    )
    return spread.reshape(rows * group, heads, width)


def pair_scores(query_sel, key_all):
    scale = query_sel.shape[-1] ** (-0.5)
    return (
        jnp.einsum("qhd,khd->hqk", query_sel, key_all, preferred_element_type=jnp.float32) * scale
    )


def attend(query_sel, key_all, value_all):
    scores = pair_scores(query_sel, key_all)
    level_max = jnp.max(scores, axis=-1)
    raw = jnp.exp(scores - level_max[..., None])
    level_total = jnp.sum(raw, axis=-1)
    weights = raw.astype(jnp.bfloat16)
    level_sum = jnp.einsum("hqk,khd->qhd", weights, value_all, preferred_element_type=jnp.float32)
    return (level_max.T, level_total.T, level_sum)


def attend_back(query_sel, grad_sel, log_sel, delta_sel, key_all, value_all):
    scale = query_sel.shape[-1] ** (-0.5)
    scores = pair_scores(query_sel, key_all)
    probs = jnp.exp(scores - log_sel.T[:, :, None])
    grad_probs = jnp.einsum("qhd,khd->hqk", grad_sel, value_all, preferred_element_type=jnp.float32)
    low_scores = (probs * (grad_probs - delta_sel.T[:, :, None])).astype(jnp.bfloat16)
    low_probs = probs.astype(jnp.bfloat16)
    grad_value = jnp.einsum("hqk,qhd->khd", low_probs, grad_sel, preferred_element_type=jnp.float32)
    grad_key = (
        jnp.einsum("hqk,qhd->khd", low_scores, query_sel, preferred_element_type=jnp.float32)
        * scale
    )
    grad_query = (
        jnp.einsum("hqk,khd->qhd", low_scores, key_all, preferred_element_type=jnp.float32) * scale
    )
    return (grad_query, grad_key, grad_value)


def bit_count(count):
    return count.bit_length() - 1


def join_pair(mine, partner, position, bit):
    upper = position >> bit & 1
    return jnp.where(
        upper == 1, jnp.concatenate([partner, mine], 0), jnp.concatenate([mine, partner], 0)
    )


def split_pair(buffer, position, bit):
    half = buffer.shape[0] // 2
    upper = position >> bit & 1
    lower_part = buffer[:half]
    upper_part = buffer[half:]
    outgoing = jnp.where(upper == 1, lower_part, upper_part)
    kept = jnp.where(upper == 1, upper_part, lower_part)
    return (outgoing, kept)


def near_collect(piece, position):
    for bit in range(2):
        partner = swapped(piece, "seq", bit)
        piece = join_pair(piece, partner, position, bit)
    return piece


def mid_collect(piece, position, count):
    for bit in range(bit_count(count) - 2):
        partner = swapped(piece, "seq", bit)
        piece = join_pair(piece, partner, position, bit)
    return piece


def near_return(buffer, position):
    for bit in reversed(range(2)):
        outgoing, kept = split_pair(buffer, position, bit)
        buffer = kept + swapped(outgoing.astype(jnp.bfloat16), "seq", bit).astype(outgoing.dtype)
    return buffer


def mid_return(buffer, position, count):
    for bit in reversed(range(bit_count(count) - 2)):
        outgoing, kept = split_pair(buffer, position, bit)
        buffer = kept + swapped(outgoing.astype(jnp.bfloat16), "seq", bit).astype(outgoing.dtype)
    return buffer


def on_device(queries, key_states, value_states, grad_output, head_offsets):
    tok_rows = queries.shape[0]
    heads = head_offsets.shape[1]
    width = queries.shape[1] // heads
    count = lax.axis_size("seq")
    position = lax.axis_index("seq")
    groups = (1, 4, count // 4, count)
    query3 = queries.reshape(tok_rows, heads, width)
    key3 = key_states.reshape(tok_rows, heads, width)
    value3 = value_states.reshape(tok_rows, heads, width)
    grad3 = grad_output.reshape(tok_rows, heads, width)
    picks = []
    for level in range(4):
        offset_row = head_offsets[level]
        picks.append(
            (
                pick_rows(query3, groups[level], offset_row),
                jnp.concatenate(
                    [
                        pick_rows(key3, groups[level], offset_row),
                        pick_rows(value3, groups[level], offset_row),
                    ],
                    axis=2,
                ),
            )
        )
    payloads = [picks[level][1] for level in range(1, 4)]
    gathered = [
        near_collect(payloads[0], position),
        mid_collect(payloads[1], position, count),
        lax.all_gather(payloads[2], "seq", axis=0, tiled=True),
    ]
    level_pairs = [picks[0][1]] + list(gathered)
    stats = []
    for level in range(4):
        group = groups[level]
        offset_row = head_offsets[level]
        pair = level_pairs[level]
        row_max, row_total, row_sum = attend(picks[level][0], pair[..., :width], pair[..., width:])
        stats.append(
            (
                place_rows(row_max[..., None], group, offset_row, NEG_FILL)[..., 0],
                place_rows(row_total[..., None], group, offset_row, 0.0)[..., 0],
                place_rows(row_sum, group, offset_row, 0.0),
            )
        )
    top_max = stats[0][0]
    for item in stats[1:]:
        top_max = jnp.maximum(top_max, item[0])
    total = jnp.zeros_like(top_max)
    combined = jnp.zeros((tok_rows, heads, width), jnp.float32)
    for item in stats:
        factor = jnp.exp(item[0] - top_max)
        total = total + factor * item[1]
        combined = combined + factor[..., None] * item[2]
    attended3 = (combined / total[..., None]).astype(jnp.bfloat16)
    log_total = top_max + jnp.log(total)
    delta = jnp.sum(grad3.astype(jnp.float32) * attended3.astype(jnp.float32), axis=-1)
    grad_query = jnp.zeros((tok_rows, heads, width), jnp.float32)
    grad_key = jnp.zeros((tok_rows, heads, width), jnp.float32)
    grad_value = jnp.zeros((tok_rows, heads, width), jnp.float32)
    returned = []
    query_sends = []
    for level in range(4):
        group = groups[level]
        offset_row = head_offsets[level]
        pair = level_pairs[level]
        grad_pick = pick_rows(grad3, group, offset_row)
        log_pick = pick_rows(log_total[..., None], group, offset_row)[..., 0]
        delta_pick = pick_rows(delta[..., None], group, offset_row)[..., 0]
        query_part, key_part, value_part = attend_back(
            picks[level][0], grad_pick, log_pick, delta_pick, pair[..., :width], pair[..., width:]
        )
        grad_query = grad_query + place_rows(query_part, group, offset_row, 0.0)
        if level == 0:
            grad_key = place_rows(key_part, group, offset_row, 0.0)
            grad_value = place_rows(value_part, group, offset_row, 0.0)
        else:
            returned.append(jnp.concatenate([key_part, value_part], axis=2))
            query_sends.append(
                (
                    jnp.concatenate([picks[level][0], grad_pick], axis=2),
                    jnp.concatenate([log_pick, delta_pick], axis=1),
                )
            )
    owned = [
        near_return(returned[0], position),
        mid_return(returned[1], position, count),
        lax.psum_scatter(returned[2], "seq", scatter_dimension=0, tiled=True),
    ]
    for level in range(1, 4):
        group = groups[level]
        offset_row = head_offsets[level]
        mine = owned[level - 1]
        grad_key = grad_key + place_rows(mine[..., :width], group, offset_row, 0.0)
        grad_value = grad_value + place_rows(mine[..., width:], group, offset_row, 0.0)
    full = heads * width
    return (
        attended3.reshape(tok_rows, full),
        grad_query.reshape(tok_rows, full).astype(jnp.bfloat16),
        grad_key.reshape(tok_rows, full).astype(jnp.bfloat16),
        grad_value.reshape(tok_rows, full).astype(jnp.bfloat16),
    )


def solution(mesh):
    placed = (
        P(("dp", "seq"), None),
        P(("dp", "seq"), None),
        P(("dp", "seq"), None),
        P(("dp", "seq"), None),
        P(),
    )
    return jax.shard_map(
        on_device,
        mesh=mesh,
        in_specs=placed,
        out_specs=(
            P(("dp", "seq"), None),
            P(("dp", "seq"), None),
            P(("dp", "seq"), None),
            P(("dp", "seq"), None),
        ),
        check_vma=False,
    )
```

profile of v0, /device:TPU:6, one launch (start us, length us, event | category | flops | bytes accessed | tf_op | source)
XLA Modules:
  0.0 464.3 jit_solution(7739069431102516425)
XLA Ops:
  14.2 1.9 collective-permute-start.2
  20.2 2.4 collective-permute-start
  24.7 4.0 fusion.26
  29.0 84.8 %all_gather.3 = bf16[128,12,128]{2,1,0:T(8,128)(2,1)S(1)} all-gather(bf16[2,12,128]{2,1,0:T(8,128)(2,1)S(1)} %copy.402), channel_id=1, replica_groups=mesh['seq'=64,'dp'=8] {'seq'}, dimensions={0}, use_global_device_ids=true | all-gather | bytes 399360 | tf_op jit(solution)/shard_map/all_gather | solution.py:143
  117.5 2.1 collective-permute-start.3
  131.0 2.1 collective-permute-start.4
  134.8 3.9 collective-permute-start.1
  139.4 14.4 %collective-permute-done.4 = bf16[32,12,128]{0,2,1:T(8,128)(2,1)S(1)} collective-permute-done((bf16[32,12,128]{0,2,1:T(8,128)(2,1)S(1)}, bf16[32,12,128]{0,2,1:T(8,128)(2,1)S(1)}, u32[]{:S(2)}, u32[]{:S(2)}) %collective-permute-start.4) | collective-permute-done | bytes 98336 | tf_op jit(solution)/shard_map/ppermute | solution.py:10
  155.0 2.0 collective-permute-start.5
  165.3 30.0 %collective-permute-done.5 = bf16[64,12,128]{0,2,1:T(8,128)(2,1)} collective-permute-done((bf16[64,12,128]{0,2,1:T(8,128)(2,1)}, bf16[64,12,128]{0,2,1:T(8,128)(2,1)}, u32[]{:S(2)}, u32[]{:S(2)}) %collective-permute-start.5) | collective-permute-done | bytes 196640 | tf_op jit(solution)/shard_map/ppermute | solution.py:10
  227.3 1.9 collective-permute-start.6
  233.3 2.1 collective-permute-start.8
  237.8 2.0 copy.475
  249.8 2.0 copy.425
  251.8 2.3 divide_convert_fusion.1
  254.1 18.5 %collective-permute-done.8 = bf16[64,12,128]{0,2,1:T(8,128)(2,1)} collective-permute-done((bf16[64,12,128]{0,2,1:T(8,128)(2,1)}, bf16[64,12,128]{0,2,1:T(8,128)(2,1)}, u32[]{:S(2)}, u32[]{:S(2)}) %collective-permute-start.8) | collective-permute-done | bytes 196640 | tf_op jit(solution)/shard_map/ppermute | solution.py:10
  274.1 1.9 collective-permute-start.9
  277.5 1.9 collective-permute-start.7
  279.4 12.9 %collective-permute-done.9 = bf16[32,12,128]{0,2,1:T(8,128)(2,1)S(1)} collective-permute-done((bf16[32,12,128]{0,2,1:T(8,128)(2,1)S(1)}, bf16[32,12,128]{0,2,1:T(8,128)(2,1)S(1)}, u32[]{:S(2)}, u32[]{:S(2)}) %collective-permute-start.9) | collective-permute-done | bytes 98336 | tf_op jit(solution)/shard_map/ppermute | solution.py:10
  292.8 1.9 collective-permute-start.10
  295.0 10.7 %collective-permute-done.10 = bf16[16,12,128]{0,2,1:T(8,128)(2,1)S(1)} collective-permute-done((bf16[16,12,128]{0,2,1:T(8,128)(2,1)S(1)}, bf16[16,12,128]{0,2,1:T(8,128)(2,1)S(1)}, u32[]{:S(2)}, u32[]{:S(2)}) %collective-permute-start.10) | collective-permute-done | bytes 49184 | tf_op jit(solution)/shard_map/ppermute | solution.py:10
  306.2 1.9 collective-permute-start.11
  313.9 135.3 %reduce-scatter.2.cloned.1.call-done = f32[2,12,128]{2,1,0:T(8,128)} async-done(((f32[128,12,128]{2,1,0:T(8,128)}), f32[2,12,128]{2,1,0:T(8,128)}) %reduce-scatter.2.cloned.1.call-update) | async-done | bytes 12304 | tf_op jit(solution)/shard_map/reduce_scatter | solution.py:201
  454.8 2.7 add_convert_fusion
  (446 shorter events, 102.8 us)
Async XLA Ops:
  7.2 442.1 %reduce-scatter.2.cloned.1.call-start = ((), (), s32[]{:S(2)}) async-start(), calls=%async_computation.1 | async-start | bytes 1064960 | tf_op jit(solution)/shard_map/reduce_scatter | solution.py:201
  8.0 116.7 %copy-start.95 = (pred[16,12]{1,0:T(8,128)(4,1)}, pred[16,12]{1,0:T(8,128)(4,1)S(1)}, u32[]{:S(2)}) copy-start(pred[16,12]{1,0:T(8,128)(4,1)S(1)} %iota_compare_fusion.1) | copy-start | bytes 580
  14.2 102.0 %collective-permute-start.2 = (bf16[8,12,128]{2,0,1:T(8,128)(2,1)}, bf16[8,12,128]{2,0,1:T(8,128)(2,1)}, u32[]{:S(2)}, u32[]{:S(2)}) collective-permute-start(bf16[8,12,128]{2,0,1:T(8,128)(2,1)} %pad_maximum_fusion.7), channel_id=1, source_target_pairs={{0,8},{8,0},{16,24},{24,16},{32,40},{40,32},{48,56},{56,48},{64,72... | collective-permute-start | bytes 73736 | tf_op jit(solution)/shard_map/ppermute | solution.py:10
  17.4 107.4 %copy-start.116 = (pred[4,12]{1,0:T(4,128)(4,1)}, pred[4,12]{1,0:T(4,128)(4,1)S(1)}, u32[]{:S(2)}) copy-start(pred[4,12]{1,0:T(4,128)(4,1)S(1)} %iota_compare_fusion.2) | copy-start | bytes 148
  20.2 112.9 %collective-permute-start = (bf16[32,12,128]{0,2,1:T(8,128)(2,1)}, bf16[32,12,128]{0,2,1:T(8,128)(2,1)}, u32[]{:S(2)}, u32[]{:S(2)}) collective-permute-start(bf16[32,12,128]{0,2,1:T(8,128)(2,1)} %pad_maximum_fusion.3), channel_id=1, source_target_pairs={{0,8},{8,0},{16,24},{24,16},{32,40},{40,32},{48,56},{56,48},{64,72... | collective-permute-start | bytes 294920 | tf_op jit(solution)/shard_map/ppermute | solution.py:10
  23.9 91.5 %copy-start.77 = (pred[12]{0:T(512)(128)(4,1)}, pred[12]{0:T(512)(128)(4,1)S(1)}, u32[]{:S(2)}) copy-start(pred[12]{0:T(512)(128)(4,1)S(1)} %compare_bitcast_fusion) | copy-start | bytes 40
  28.7 86.1 %copy-start.14 = (bf16[2,12,64]{0,2,1:T(8,128)(2,1)}, bf16[2,12,64]{0,2,1:T(8,128)(2,1)S(1)}, u32[]{:S(2)}) copy-start(bf16[2,12,64]{0,2,1:T(8,128)(2,1)S(1)} %get-tuple-element.15) | copy-start | bytes 9220
  115.8 22.9 %copy-start.67 = (f32[12,128]{1,0:T(8,128)}, f32[12,128]{1,0:T(8,128)S(1)}, u32[]{:S(2)}) copy-start(f32[12,128]{1,0:T(8,128)S(1)} %get-tuple-element.57) | copy-start | bytes 18436
  117.5 12.9 %collective-permute-start.3 = (bf16[16,12,128]{2,0,1:T(8,128)(2,1)S(1)}, bf16[16,12,128]{2,0,1:T(8,128)(2,1)S(1)}, u32[]{:S(2)}, u32[]{:S(2)}) collective-permute-start(bf16[16,12,128]{2,0,1:T(8,128)(2,1)S(1)} %maximum_select_fusion.4), channel_id=1, source_target_pairs={{0,16},{8,24},{16,0},{24,8},{32,48},{40,56},{48,32},{56,40},{64,80... | collective-permute-start | bytes 147464 | tf_op jit(solution)/shard_map/ppermute | solution.py:10
  131.0 22.8 %collective-permute-start.4 = (bf16[32,12,128]{0,2,1:T(8,128)(2,1)S(1)}, bf16[32,12,128]{0,2,1:T(8,128)(2,1)S(1)}, u32[]{:S(2)}, u32[]{:S(2)}) collective-permute-start(bf16[32,12,128]{0,2,1:T(8,128)(2,1)S(1)} %broadcast_select_fusion.4), channel_id=1, source_target_pairs={{0,32},{8,40},{16,48},{24,56},{32,0},{40,8},{48,16},{56,24},{64,96... | collective-permute-start | bytes 294920 | tf_op jit(solution)/shard_map/ppermute | solution.py:10
  134.8 22.3 %collective-permute-start.1 = (bf16[64,12,128]{0,2,1:T(8,128)(2,1)S(1)}, bf16[64,12,128]{0,2,1:T(8,128)(2,1)S(1)}, u32[]{:S(2)}, u32[]{:S(2)}) collective-permute-start(bf16[64,12,128]{0,2,1:T(8,128)(2,1)S(1)} %maximum_select_fusion), channel_id=1, source_target_pairs={{0,16},{8,24},{16,0},{24,8},{32,48},{40,56},{48,32},{56,40},{64,80... | collective-permute-start | bytes 589832 | tf_op jit(solution)/shard_map/ppermute | solution.py:10
  155.0 40.3 %collective-permute-start.5 = (bf16[64,12,128]{0,2,1:T(8,128)(2,1)}, bf16[64,12,128]{0,2,1:T(8,128)(2,1)}, u32[]{:S(2)}, u32[]{:S(2)}) collective-permute-start(bf16[64,12,128]{0,2,1:T(8,128)(2,1)} %maximum_select_fusion.2), channel_id=1, source_target_pairs={{0,64},{8,72},{16,80},{24,88},{32,96},{40,104},{48,112},{56,120},{... | collective-permute-start | bytes 589832 | tf_op jit(solution)/shard_map/ppermute | solution.py:10
  165.3 31.8 %copy-start.60 = (bf16[8,12,64]{2,1,0:T(8,128)(2,1)S(1)}, bf16[8,12,64]{2,1,0:T(8,128)(2,1)}, u32[]{:S(2)}) copy-start(bf16[8,12,64]{2,1,0:T(8,128)(2,1)} %get-tuple-element.9) | copy-start | bytes 36868
  199.0 6.2 %copy-start.71 = (f32[8,12]{1,0:T(8,128)}, f32[8,12]{1,0:T(8,128)S(1)}, u32[]{:S(2)}) copy-start(f32[8,12]{1,0:T(8,128)S(1)} %copy.423) | copy-start | bytes 1156
  199.1 6.1 %copy-start.73 = (f32[8,12]{1,0:T(8,128)}, f32[8,12]{1,0:T(8,128)S(1)}, u32[]{:S(2)}) copy-start(f32[8,12]{1,0:T(8,128)S(1)} %copy.397) | copy-start | bytes 1156
  200.1 6.4 %copy-start.31 = (f32[128,12]{1,0:T(8,128)}, f32[128,12]{1,0:T(8,128)S(1)}, u32[]{:S(2)}) copy-start(f32[128,12]{1,0:T(8,128)S(1)} %copy.431) | copy-start | bytes 18436
  204.3 9.5 %copy-start.33 = (f32[128,12]{1,0:T(8,128)}, f32[128,12]{1,0:T(8,128)S(1)}, u32[]{:S(2)}) copy-start(f32[128,12]{1,0:T(8,128)S(1)} %copy.442) | copy-start | bytes 18436
  205.1 8.7 %copy-start.35 = (f32[128,12]{1,0:T(8,128)}, f32[128,12]{1,0:T(8,128)S(1)}, u32[]{:S(2)}) copy-start(f32[128,12]{1,0:T(8,128)S(1)} %copy.436) | copy-start | bytes 18436
  227.3 48.7 %collective-permute-start.6 = (bf16[64,12,128]{0,2,1:T(8,128)(2,1)}, bf16[64,12,128]{0,2,1:T(8,128)(2,1)}, u32[]{:S(2)}, u32[]{:S(2)}) collective-permute-start(bf16[64,12,128]{0,2,1:T(8,128)(2,1)} %select_convert_fusion.5), channel_id=1, source_target_pairs={{0,16},{8,24},{16,0},{24,8},{32,48},{40,56},{48,32},{56,40},{64,80... | collective-permute-start | bytes 589832 | tf_op jit(solution)/shard_map/ppermute | solution.py:10
  233.3 39.4 %collective-permute-start.8 = (bf16[64,12,128]{0,2,1:T(8,128)(2,1)}, bf16[64,12,128]{0,2,1:T(8,128)(2,1)}, u32[]{:S(2)}, u32[]{:S(2)}) collective-permute-start(bf16[64,12,128]{0,2,1:T(8,128)(2,1)} %select_convert_fusion.3), channel_id=1, source_target_pairs={{0,64},{8,72},{16,80},{24,88},{32,96},{40,104},{48,112},{56,120},{... | collective-permute-start | bytes 589832 | tf_op jit(solution)/shard_map/ppermute | solution.py:10
  274.1 18.2 %collective-permute-start.9 = (bf16[32,12,128]{0,2,1:T(8,128)(2,1)S(1)}, bf16[32,12,128]{0,2,1:T(8,128)(2,1)S(1)}, u32[]{:S(2)}, u32[]{:S(2)}) collective-permute-start(bf16[32,12,128]{0,2,1:T(8,128)(2,1)S(1)} %select_convert_fusion.2), channel_id=1, source_target_pairs={{0,32},{8,40},{16,48},{24,56},{32,0},{40,8},{48,16},{56,24},{64,96... | collective-permute-start | bytes 294920 | tf_op jit(solution)/shard_map/ppermute | solution.py:10
  277.5 17.2 %collective-permute-start.7 = (bf16[32,12,128]{0,2,1:T(8,128)(2,1)S(1)}, bf16[32,12,128]{0,2,1:T(8,128)(2,1)S(1)}, u32[]{:S(2)}, u32[]{:S(2)}) collective-permute-start(bf16[32,12,128]{0,2,1:T(8,128)(2,1)S(1)} %select_convert_fusion.4), channel_id=1, source_target_pairs={{0,8},{8,0},{16,24},{24,16},{32,40},{40,32},{48,56},{56,48},{64,72... | collective-permute-start | bytes 294920 | tf_op jit(solution)/shard_map/ppermute | solution.py:10
  292.8 12.9 %collective-permute-start.10 = (bf16[16,12,128]{0,2,1:T(8,128)(2,1)S(1)}, bf16[16,12,128]{0,2,1:T(8,128)(2,1)S(1)}, u32[]{:S(2)}, u32[]{:S(2)}) collective-permute-start(bf16[16,12,128]{0,2,1:T(8,128)(2,1)S(1)} %select_convert_fusion.1), channel_id=1, source_target_pairs={{0,16},{8,24},{16,0},{24,8},{32,48},{40,56},{48,32},{56,40},{64,80... | collective-permute-start | bytes 147464 | tf_op jit(solution)/shard_map/ppermute | solution.py:10
  306.2 4.7 %collective-permute-start.11 = (bf16[8,12,128]{0,2,1:T(8,128)(2,1)S(1)}, bf16[8,12,128]{0,2,1:T(8,128)(2,1)S(1)}, u32[]{:S(2)}, u32[]{:S(2)}) collective-permute-start(bf16[8,12,128]{0,2,1:T(8,128)(2,1)S(1)} %select_convert_fusion), channel_id=1, source_target_pairs={{0,8},{8,0},{16,24},{24,16},{32,40},{40,32},{48,56},{56,48},{64,72... | collective-permute-start | bytes 73736 | tf_op jit(solution)/shard_map/ppermute | solution.py:10
  (108 other events, 147.5 us)
Sparse Core Ops, SparseCore 0:
  242.4 206.7 reduce-scatter.1
where the time goes:
time: 466 us; the launch traced here: 464 us
  waiting for transfers between devices  222 us (48%)
  blocking collectives  84.8 us (18%)
  local copies, waits for them, and re-layouts  70.1 us (15%)
  other arithmetic  32.8 us (7%)
  starting transfers between devices  26.2 us (6%)
  between operations  15.7 us (3%)
  matrix products  12.7 us (3%)
    reduce_scatter x1, waiting for transfers between devices, on_device(): lax.psum_scatter(returned[2], 'seq', scatter_dimension=0, tiled=True)  135 us
    ppermute x12, waiting for transfers between devices, swapped(): lax.ppermute(value, axis, [(i, i ^ 1 << stride) for i in range(lax.axis_s...  86.6 us
    all_gather x1, blocking collectives, on_device(): lax.all_gather(payloads[2], 'seq', axis=0, tiled=True)  84.8 us
    broadcast_in_dim x58, local copies, waits for them, and re-layouts, place_rows(): jnp.where(onehot[None, :, :, None], picked[:, None, :, :], jnp.asarray(fi...  26.8 us
    ppermute x12, starting transfers between devices, swapped(): lax.ppermute(value, axis, [(i, i ^ 1 << stride) for i in range(lax.axis_s...  26.2 us
    unnamed x247, local copies, waits for them, and re-layouts  17.8 us
  transfers between devices with their start and end apart: 13, of which 6 were waited for; matrix products, arithmetic and copies ran while one was open for 14% of the time, Pallas kernels for 0%

commit v1 on v0

v1 whole, which is shorter than its diff:
```python
import functools

import jax
import jax.numpy as jnp
from jax import lax
from jax.experimental import pallas as pl
from jax.experimental.pallas import tpu as pltpu
from jax.sharding import Mesh, PartitionSpec as P

HEADS = 12
WIDTH = 64
TOK = 128
FULL = HEADS * WIDTH
PAIRS = HEADS // 2
SCALE = WIDTH ** -0.5
GROUPS = (1, 4, 16, 64)
PARTS = (("yh", 2), ("zh", 2), ("zm", 4), ("zl", 2), ("c", 2))
FAR = ("yh", "zh", "zm")
NEAR = ("zl", "c")
N_FAR = 16
N_NEAR = 4
ROWS1, ROWS2, ROWS3 = 32, 8, 2
NEG = -1e30
F32 = jnp.float32
BF16 = jnp.bfloat16
VMEM = pl.BlockSpec(memory_space=pltpu.VMEM)
SMEM = pl.BlockSpec(memory_space=pltpu.SMEM)
PARAMS = pltpu.CompilerParams(vmem_limit_bytes=48 * 1024 * 1024)


def iota(shape, dim):
    return lax.broadcasted_iota(jnp.int32, shape, dim)


def dot(a, b):
    return lax.dot_general(a, b, (((1,), (0,)), ((), ())), preferred_element_type=F32)


def dot_t(a, b):
    return lax.dot_general(a, b, (((1,), (1,)), ((), ())), preferred_element_type=F32)


def lanes(pair):
    return slice(pair * 128, (pair + 1) * 128)


def halves(value):
    n = value.shape[0] // 2
    return jnp.where(iota((n, 128), 1) < WIDTH, value[:n], value[n:])


def stacked(value):
    low = iota(value.shape, 1) < WIDTH
    zero = jnp.zeros_like(value)
    return jnp.concatenate([jnp.where(low, value, zero), jnp.where(low, zero, value)], 0)


def pick_kernel(off_ref, k_ref, v_ref, q_ref, g_ref, near_ref, mid_ref, far_ref):
    refs = (k_ref, v_ref, q_ref, g_ref)
    row = iota((48, TOK), 0)
    tok = iota((48, TOK), 1)
    base = jnp.where(row < 32, row * 4, jnp.where(row < 40, (row - 32) * 16, (row % 2) * 64))

    def selector(head, array):
        off = jnp.where(
            row < 32, off_ref[1, head], jnp.where(row < 40, off_ref[2, head], off_ref[3, head])
        )
        live = (row < 40) | ((row - 40) // 2 == array)
        return jnp.where((tok == base + off) & live, 1.0, 0.0).astype(BF16)

    for pair in range(PAIRS):
        picked = []
        for array in range(4):
            choose = jnp.concatenate(
                [selector(2 * pair, array), selector(2 * pair + 1, array)], 0
            )
            picked.append(halves(dot(choose, refs[array][:, lanes(pair)])))
        near_ref[:, lanes(pair)] = jnp.concatenate([x[:32] for x in picked], 0).astype(BF16)
        mid_ref[:, lanes(pair)] = jnp.concatenate([x[32:40] for x in picked], 0).astype(BF16)
        far = picked[0][40:] + picked[1][40:] + picked[2][40:] + picked[3][40:]
        far_ref[:, lanes(pair)] = far.astype(BF16)


def split_kernel(far_ref, mid_ref, kv_ref, qg_ref):
    both = jnp.concatenate([far_ref[...], mid_ref[...]], 0)
    row = iota((128, 256), 0)
    col = iota((128, 256), 1)
    run = row // 32
    slot = row % 32
    for first, out_ref in ((0, kv_ref), (2, qg_ref)):
        array = first + run // 2
        far_col = slot // 2 * 8 + array * 2 + slot % 2
        mid_col = 128 + slot // 8 * 32 + array * 8 + slot % 8
        choose = jnp.where(col == jnp.where(run % 2 == 0, far_col, mid_col), 1.0, 0.0)
        out_ref[...] = dot(choose.astype(BF16), both).astype(BF16)


def gathered(own_ref, near_ref, back_ref, array, pair):
    cols = lanes(pair)
    one = [near_ref[d * 128 + array * 32 : d * 128 + array * 32 + 32, cols] for d in range(N_NEAR)]
    half = (array % 2) * 64
    three = [back_ref[d * 128 + half : d * 128 + half + 32, cols] for d in range(N_NEAR)]
    two = [back_ref[d * 128 + half + 32 : d * 128 + half + 64, cols] for d in range(N_NEAR)]
    return jnp.concatenate([own_ref[:, cols]] + one + two + three, 0)


def chosen(off_ref, head, level):
    return (iota((TOK, 1), 0) & (GROUPS[level] - 1)) == off_ref[level, head]


def forward_kernel(
    off_ref, k_ref, v_ref, q_ref, g_ref, near_ref, back_ref, att_ref, gq_ref, stat_ref, own_ref
):
    tok = iota((TOK, 128), 0)
    lane = iota((1, 128), 1)
    eye = tok == iota((TOK, 128), 1)
    sums = [None] * 8
    for pair in range(PAIRS):
        keys = gathered(k_ref, near_ref, back_ref, 0, pair)
        values = gathered(v_ref, near_ref, back_ref, 1, pair)
        grad = stacked(g_ref[:, lanes(pair)])
        scores = dot_t(stacked(q_ref[:, lanes(pair)]), keys) * SCALE
        live = [
            jnp.concatenate(
                [chosen(off_ref, 2 * pair, level), chosen(off_ref, 2 * pair + 1, level)], 0
            )
            for level in range(1, 4)
        ]
        blocks = [scores[:, level * 128 : level * 128 + 128] for level in range(4)]
        top = blocks[0]
        for level in range(1, 4):
            top = jnp.maximum(top, jnp.where(live[level - 1], blocks[level], NEG))
        top = jnp.max(top, axis=1, keepdims=True)
        raw = [jnp.exp(blocks[0] - top)]
        for level in range(1, 4):
            raw.append(jnp.exp(blocks[level] - jnp.where(live[level - 1], top, -NEG)))
        total = jnp.sum(raw[0] + raw[1] + raw[2] + raw[3], axis=1, keepdims=True)
        inverse = 1.0 / total
        raw = jnp.concatenate(raw, 1)
        out = halves(dot(raw.astype(BF16), values) * inverse).astype(BF16)
        att_ref[:, lanes(pair)] = out
        out = out.astype(F32)
        delta = jnp.sum(grad.astype(F32) * jnp.concatenate([out, out], 0), axis=1, keepdims=True)
        grad_probs = dot_t(grad, values)
        grad_scores = (raw * inverse * (grad_probs - delta)).astype(BF16)
        gq_ref[:, lanes(pair)] = halves(dot(grad_scores, keys) * SCALE).astype(BF16)
        logs = top + jnp.log(total)
        for side in range(2):
            head = 2 * pair + side
            turn = head // 4
            one = lane - 32 * turn
            two = lane - 96 - 8 * turn
            three = lane - 120 - 2 * turn
            source = jnp.where(
                (one >= 0) & (one < 32),
                one * 4 + off_ref[1, head],
                jnp.where(
                    (two >= 0) & (two < 8),
                    two * 16 + off_ref[2, head],
                    jnp.where(
                        (three >= 0) & (three < 2), three * 64 + off_ref[3, head], -1
                    ),
                ),
            )
            hit = tok == source
            for kind, column in enumerate((logs, delta)):
                column = column[side * TOK : side * TOK + TOK]
                own_ref[2 * head + kind : 2 * head + kind + 1, :] = jnp.sum(
                    jnp.where(eye, column, 0.0), axis=0, keepdims=True
                )
                line = jnp.sum(jnp.where(hit, column, 0.0), axis=0, keepdims=True)
                place = 2 * (head % 4) + kind
                sums[place] = line if sums[place] is None else sums[place] + line
    stat_ref[...] = jnp.concatenate(sums, 0)


def backward_kernel(
    off_ref, where_ref, k_ref, v_ref, q_ref, g_ref, near_ref, back_ref, own_ref, stat_ref,
    gk_ref, gv_ref, line_ref,
):
    lane = iota((8, 128), 1)
    mine = where_ref[0]

    def block(d, peer):
        return stat_ref[pl.ds(pl.multiple_of((d * N_FAR + peer) * 8, 8), 8), :]

    zero = jnp.zeros((8, 128), F32)
    acc = [[zero] * 3 for _ in range(3)]

    def put(level, value, at, width, start):
        inside = (lane >= at) & (lane < at + width)
        for turn in range(3):
            moved = pltpu.roll(value, (at - start - width * turn) % 128, 1)
            acc[level][turn] = jnp.where(inside, moved, acc[level][turn])

    for d in range(N_NEAR):
        put(0, block(d, mine), d * 32, 32, 0)
        for slot, step in enumerate((0, 2, 1, 3)):
            put(1, block(d, mine ^ step), d * 32 + slot * 8, 8, 96)
        for peer in range(N_FAR):
            put(2, block(d, peer), d * 32 + peer * 2, 2, 120)
    for level in range(3):
        for turn in range(3):
            line_ref[turn * 8 : turn * 8 + 8, level * 128 : level * 128 + 128] = acc[level][turn]

    for pair in range(PAIRS):
        queries = gathered(q_ref, near_ref, back_ref, 2, pair)
        grads = gathered(g_ref, near_ref, back_ref, 3, pair)
        scores = dot_t(stacked(k_ref[:, lanes(pair)]), queries) * SCALE
        grad_probs = dot_t(stacked(v_ref[:, lanes(pair)]), grads)
        probs, grad_scores = [], []
        for side in range(2):
            head = 2 * pair + side
            rows = slice(side * TOK, side * TOK + TOK)
            probs_row, grad_row = [], []
            for level in range(4):
                cols = slice(level * 128, level * 128 + 128)
                if level == 0:
                    log_line = own_ref[2 * head : 2 * head + 1, :]
                    delta_line = own_ref[2 * head + 1 : 2 * head + 2, :]
                else:
                    at = slice(level * 128 - 128, level * 128)
                    log_line = line_ref[2 * head : 2 * head + 1, at]
                    delta_line = line_ref[2 * head + 1 : 2 * head + 2, at]
                power = scores[rows, cols] - log_line
                if level:
                    power = jnp.where(chosen(off_ref, head, level), power, NEG)
                prob = jnp.exp(power)
                probs_row.append(prob.astype(BF16))
                grad_row.append((prob * (grad_probs[rows, cols] - delta_line)).astype(BF16))
            probs.append(jnp.concatenate(probs_row, 1))
            grad_scores.append(jnp.concatenate(grad_row, 1))
        gv_ref[:, lanes(pair)] = halves(dot(jnp.concatenate(probs, 0), grads)).astype(BF16)
        gk_ref[:, lanes(pair)] = halves(
            dot(jnp.concatenate(grad_scores, 0), queries) * SCALE
        ).astype(BF16)


def shape(*dims, dtype=BF16):
    return jax.ShapeDtypeStruct(dims, dtype)


def cost(flops, moved, exps=0):
    return pl.CostEstimate(flops=flops, bytes_accessed=moved, transcendentals=exps)


def to_far(value):
    rows, cols = value.shape
    spread = jnp.broadcast_to(value[None], (N_FAR, rows, cols)).reshape(N_FAR * rows, cols)
    return lax.all_to_all(spread, FAR, 0, 0, tiled=True)


def to_near(value):
    return lax.all_gather(value, NEAR, axis=0, tiled=True)


def swap_mid(value, step):
    return lax.ppermute(value, "zm", [(i, i ^ step) for i in range(4)])


def on_device(queries, key_states, value_states, grad_output, head_offsets):
    mine = (lax.axis_index("yh") * 2 + lax.axis_index("zh")) * 4 + lax.axis_index("zm")
    own = (key_states, value_states, queries, grad_output)
    near, mid, far = pl.pallas_call(
        pick_kernel,
        name="pick",
        out_shape=(shape(128, FULL), shape(32, FULL), shape(8, FULL)),
        in_specs=[SMEM] + [VMEM] * 4,
        out_specs=(VMEM,) * 3,
        compiler_params=PARAMS,
        cost_estimate=cost(200_000_000, 1_100_000),
    )(head_offsets, *own)
    far_rows = to_far(far)
    mid_rows = jnp.concatenate([mid, swap_mid(mid, 2)], 0)
    mid_rows = jnp.concatenate([mid_rows, swap_mid(mid_rows, 1)], 0)
    near_rows = to_near(near)
    kv_rows, qg_rows = pl.pallas_call(
        split_kernel,
        name="split",
        out_shape=(shape(128, FULL), shape(128, FULL)),
        in_specs=[VMEM] * 2,
        out_specs=(VMEM,) * 2,
        compiler_params=PARAMS,
        cost_estimate=cost(100_000_000, 800_000),
    )(far_rows, mid_rows)
    kv_rows = to_near(kv_rows)
    attended, grad_query, stats, own_stats = pl.pallas_call(
        forward_kernel,
        name="forward",
        out_shape=(
            shape(TOK, FULL),
            shape(TOK, FULL),
            shape(8, 128, dtype=F32),
            shape(2 * HEADS, 128, dtype=F32),
        ),
        in_specs=[SMEM] + [VMEM] * 6,
        out_specs=(VMEM,) * 4,
        compiler_params=PARAMS,
        cost_estimate=cost(1_000_000_000, 3_000_000, 800_000),
    )(head_offsets, *own, near_rows, kv_rows)
    all_stats = to_near(to_far(stats))
    qg_rows = to_near(qg_rows)
    grad_key, grad_value = pl.pallas_call(
        backward_kernel,
        name="backward",
        out_shape=(shape(TOK, FULL), shape(TOK, FULL)),
        in_specs=[SMEM] * 2 + [VMEM] * 8,
        out_specs=(VMEM,) * 2,
        scratch_shapes=[pltpu.VMEM((2 * HEADS, 3 * 128), F32)],
        compiler_params=PARAMS,
        cost_estimate=cost(1_000_000_000, 3_000_000, 800_000),
    )(head_offsets, mine.reshape(1), *own, near_rows, qg_rows, own_stats, all_stats)
    return attended, grad_query, grad_key, grad_value


def solution(mesh):
    names = tuple(name for name, _ in PARTS)
    sizes = tuple(size for _, size in PARTS)
    parts = Mesh(mesh.devices.reshape(sizes + mesh.devices.shape[1:]), names + ("dp",))
    rows = P(("dp",) + names, None)
    return jax.shard_map(
        on_device,
        mesh=parts,
        in_specs=(rows,) * 4 + (P(),),
        out_specs=(rows,) * 4,
        check_vma=False,
    )
```

time: 466 us -> 106 us (0.23)
  the two profiles are of different devices: /device:TPU:6 before, /device:TPU:1 now
where the time goes in v1:
time: 106 us
  starting transfers between devices  38.2 us (36%)
  blocking collectives  37.6 us (35%)
  waiting for transfers between devices  13.2 us (12%)
  Pallas kernels  10.1 us (10%)
  local copies, waits for them, and re-layouts  5.74 us (5%)
    all_gather x4, blocking collectives, to_near(): return lax.all_gather(value, NEAR, axis=0, tiled=True)  37.6 us
    all_to_all x2, starting transfers between devices, to_far(): return lax.all_to_all(spread, FAR, 0, 0, tiled=True)  29.1 us
    ppermute x2, waiting for transfers between devices, swap_mid(): return lax.ppermute(value, 'zm', [(i, i ^ step) for i in range(4)])  10 us
    ppermute x2, starting transfers between devices, swap_mid(): return lax.ppermute(value, 'zm', [(i, i ^ step) for i in range(4)])  9.14 us
    pallas_call x1, Pallas kernels, on_device(): pl.pallas_call(forward_kernel, name='forward', out_shape=(shape(TOK, FULL...  5.44 us
    unnamed x20, local copies, waits for them, and re-layouts  4.41 us
    pallas_call x1, Pallas kernels, on_device(): pl.pallas_call(backward_kernel, name='backward', out_shape=(shape(TOK, FU...  3.5 us
    all_to_all x2, waiting for transfers between devices, to_far(): return lax.all_to_all(spread, FAR, 0, 0, tiled=True)  3.14 us
  transfers between devices with their start and end apart: 4, of which 2 were waited for; matrix products, arithmetic and copies ran while one was open for 0% of the time, Pallas kernels for 0%

profile of v1, /device:TPU:1, one launch (start us, length us, event | category | flops | bytes accessed | tf_op | source)
XLA Modules:
  0.0 105.7 jit_solution(11025421365250371710)
XLA Ops:
  0.6 0.0 copy-start
  0.6 0.9 copy-done
  1.6 0.9 copy-done.2
  2.5 0.9 copy-done.4
  3.4 0.9 copy-done.6
  4.3 0.7 copy-done.8
  5.0 0.9 pick.1
  5.9 0.7 broadcast_in_dim.4
  6.6 18.4 %all-to-all-start = ((bf16[16,8,768]{2,1,0:T(8,128)(2,1)}), bf16[16,8,768]{2,1,0:T(8,128)(2,1)S(1)}, u32[]{:S(2)}, u32[]{:S(2)}) async-start(bf16[16,8,768]{2,1,0:T(8,128)(2,1)} %broadcast_in_dim.4), calls=%async_computation | async-start | bytes 393216 | tf_op jit(solution)/shard_map/all_to_all | solution.py:250
  25.0 7.2 %collective-permute-start = (bf16[32,768]{1,0:T(8,128)(2,1)S(1)}, bf16[32,768]{1,0:T(8,128)(2,1)S(1)}, u32[]{:S(2)}, u32[]{:S(2)}) collective-permute-start(bf16[32,768]{1,0:T(8,128)(2,1)S(1)} %get-tuple-element.17), channel_id=1, source_target_pairs={{0,64},{32,96},{64,0},{96,32},{1,65},{33,97},{65,1},{97,33},{2,66}... | collective-permute-start | bytes 147464 | tf_op jit(solution)/shard_map/ppermute | solution.py:258
  32.2 10.0 %collective-permute-done = bf16[32,768]{1,0:T(8,128)(2,1)S(1)} collective-permute-done((bf16[32,768]{1,0:T(8,128)(2,1)S(1)}, bf16[32,768]{1,0:T(8,128)(2,1)S(1)}, u32[]{:S(2)}, u32[]{:S(2)}) %collective-permute-start) | collective-permute-done | bytes 49184 | tf_op jit(solution)/shard_map/ppermute | solution.py:258
  42.2 2.0 %collective-permute-start.1 = (bf16[64,768]{1,0:T(8,128)(2,1)S(1)}, bf16[64,768]{1,0:T(8,128)(2,1)S(1)}, u32[]{:S(2)}, u32[]{:S(2)}) collective-permute-start(bf16[64,768]{1,0:T(8,128)(2,1)S(1)} %pad_maximum_fusion.1), channel_id=1, source_target_pairs={{0,32},{32,0},{64,96},{96,64},{1,33},{33,1},{65,97},{97,65},{2,34}... | collective-permute-start | bytes 294920 | tf_op jit(solution)/shard_map/ppermute | solution.py:258
  44.2 11.0 %all_gather.12.near_ref = bf16[512,768]{1,0:T(8,128)(2,1)S(1)} all-gather(bf16[128,768]{1,0:T(8,128)(2,1)S(1)} %get-tuple-element.15), channel_id=1, replica_groups=mesh['yh'=2,'zh'=2,'zm'=4,'zl'=2,'c'=2,'dp'=8] {'zl','c'}, dimensions={0}, use_global_device_ids=true | all-gather | bytes 983040 | tf_op jit(solution)/shard_map/all_gather | solution.py:254
  55.2 0.3 split.1
  55.5 0.0 copy-start.1
  55.5 0.0 copy-start.7
  55.6 8.9 %all_gather.13.back_ref = bf16[512,768]{1,0:T(8,128)(2,1)S(1)} all-gather(bf16[128,768]{1,0:T(8,128)(2,1)S(1)} %get-tuple-element.18), channel_id=1, replica_groups=mesh['yh'=2,'zh'=2,'zm'=4,'zl'=2,'c'=2,'dp'=8] {'zl','c'}, dimensions={0}, use_global_device_ids=true | all-gather | bytes 983040 | tf_op jit(solution)/shard_map/all_gather | solution.py:254
  64.4 5.4 %forward.1 = (bf16[128,768]{1,0:T(8,128)(2,1)}, bf16[128,768]{1,0:T(8,128)(2,1)}, f32[8,128]{1,0:T(8,128)S(1)}, f32[24,128]{1,0:T(8,128)S(1)}) custom-call(s32[4,12]{1,0:T(4,128)S(1)} %copy-done.9, bf16[128,768]{1,0:T(8,128)(2,1)S(1)} %copy-done.1, bf16[128,768]{1,0:T(8,128)(2,1)S(1)} %copy-done.3, bf16[128,768]{1,0:T(8,128)(2,1)S(1)} %copy-done.5, ...), custom_call_target="tpu_custom_call" | custom-call | flops 1000000000 | bytes 3000000 | tf_op jit(solution)/shard_map/forward/pallas_call | solution.py:287
  69.9 0.6 broadcast_in_dim.5
  70.5 10.7 %all-to-all-start.1 = ((f32[16,8,128]{2,1,0:T(8,128)}), f32[16,8,128]{2,1,0:T(8,128)S(1)}, u32[]{:S(2)}, u32[]{:S(2)}) async-start(f32[16,8,128]{2,1,0:T(8,128)} %broadcast_in_dim.5), calls=%async_computation.1 | async-start | bytes 131072 | tf_op jit(solution)/shard_map/all_to_all | solution.py:250
  81.2 10.7 %all_gather.14.back_ref = bf16[512,768]{1,0:T(8,128)(2,1)S(1)} all-gather(bf16[128,768]{1,0:T(8,128)(2,1)S(1)} %get-tuple-element.21), channel_id=1, replica_groups=mesh['yh'=2,'zh'=2,'zm'=4,'zl'=2,'c'=2,'dp'=8] {'zl','c'}, dimensions={0}, use_global_device_ids=true | all-gather | bytes 983040 | tf_op jit(solution)/shard_map/all_gather | solution.py:254
  92.0 3.1 %all-to-all-done.1 = f32[16,8,128]{2,1,0:T(8,128)S(1)} async-done(((f32[16,8,128]{2,1,0:T(8,128)}), f32[16,8,128]{2,1,0:T(8,128)S(1)}, u32[]{:S(2)}, u32[]{:S(2)}) %all-to-all-start.1) | async-done | bytes 65568 | tf_op jit(solution)/shard_map/all_to_all | solution.py:250
  95.1 7.1 %all_gather.15.stat_ref = f32[512,128]{1,0:T(8,128)S(1)} all-gather(f32[128,128]{1,0:T(8,128)S(1)} %bitcast.4), channel_id=1, replica_groups=mesh['yh'=2,'zh'=2,'zm'=4,'zl'=2,'c'=2,'dp'=8] {'zl','c'}, dimensions={0}, use_global_device_ids=true | all-gather | bytes 327680 | tf_op jit(solution)/shard_map/all_gather | solution.py:254
  102.2 3.5 %backward.1 = (bf16[128,768]{1,0:T(8,128)(2,1)}, bf16[128,768]{1,0:T(8,128)(2,1)}) custom-call(s32[4,12]{1,0:T(4,128)S(1)} %copy-done.9, s32[1]{0:T(128)} %bitcast.1.where_ref, bf16[128,768]{1,0:T(8,128)(2,1)S(1)} %copy-done.1, bf16[128,768]{1,0:T(8,128)(2,1)S(1)} %copy-done.3, bf16[128,768]{1,0:T(8,128)(2,1)S(1)} %copy-done.5, ...), custom_call_target="tpu_custom_call" | custom-call | flops 1000000000 | bytes 3000000 | tf_op jit(solution)/shard_map/backward/pallas_call | solution.py:303
  (16 shorter events, 0.1 us)
Async XLA Ops:
  0.6 0.9 copy-start
  1.6 0.9 copy-start.2
  2.5 0.9 copy-start.4
  3.4 0.9 copy-start.6
  4.3 0.7 copy-start.8
  6.6 48.6 %all-to-all-start = ((bf16[16,8,768]{2,1,0:T(8,128)(2,1)}), bf16[16,8,768]{2,1,0:T(8,128)(2,1)S(1)}, u32[]{:S(2)}, u32[]{:S(2)}) async-start(bf16[16,8,768]{2,1,0:T(8,128)(2,1)} %broadcast_in_dim.4), calls=%async_computation | async-start | bytes 393216 | tf_op jit(solution)/shard_map/all_to_all | solution.py:250
  25.0 17.2 %collective-permute-start = (bf16[32,768]{1,0:T(8,128)(2,1)S(1)}, bf16[32,768]{1,0:T(8,128)(2,1)S(1)}, u32[]{:S(2)}, u32[]{:S(2)}) collective-permute-start(bf16[32,768]{1,0:T(8,128)(2,1)S(1)} %get-tuple-element.17), channel_id=1, source_target_pairs={{0,64},{32,96},{64,0},{96,32},{1,65},{33,97},{65,1},{97,33},{2,66}... | collective-permute-start | bytes 147464 | tf_op jit(solution)/shard_map/ppermute | solution.py:258
  42.2 12.9 %collective-permute-start.1 = (bf16[64,768]{1,0:T(8,128)(2,1)S(1)}, bf16[64,768]{1,0:T(8,128)(2,1)S(1)}, u32[]{:S(2)}, u32[]{:S(2)}) collective-permute-start(bf16[64,768]{1,0:T(8,128)(2,1)S(1)} %pad_maximum_fusion.1), channel_id=1, source_target_pairs={{0,32},{32,0},{64,96},{96,64},{1,33},{33,1},{65,97},{97,65},{2,34}... | collective-permute-start | bytes 294920 | tf_op jit(solution)/shard_map/ppermute | solution.py:258
  55.5 8.9 %copy-start.1 = (bf16[128,768]{1,0:T(8,128)(2,1)S(1)}, bf16[128,768]{1,0:T(8,128)(2,1)}, u32[]{:S(2)}) copy-start(bf16[128,768]{1,0:T(8,128)(2,1)} %k_ref.5) | copy-start | bytes 589828
  55.5 8.9 %copy-start.3 = (bf16[128,768]{1,0:T(8,128)(2,1)S(1)}, bf16[128,768]{1,0:T(8,128)(2,1)}, u32[]{:S(2)}) copy-start(bf16[128,768]{1,0:T(8,128)(2,1)} %v_ref.5) | copy-start | bytes 589828
  55.5 8.9 %copy-start.5 = (bf16[128,768]{1,0:T(8,128)(2,1)S(1)}, bf16[128,768]{1,0:T(8,128)(2,1)}, u32[]{:S(2)}) copy-start(bf16[128,768]{1,0:T(8,128)(2,1)} %q_ref.5) | copy-start | bytes 589828
  55.5 8.9 %copy-start.7 = (bf16[128,768]{1,0:T(8,128)(2,1)S(1)}, bf16[128,768]{1,0:T(8,128)(2,1)}, u32[]{:S(2)}) copy-start(bf16[128,768]{1,0:T(8,128)(2,1)} %g_ref.5) | copy-start | bytes 589828
  55.6 8.9 %copy-start.9 = (s32[4,12]{1,0:T(4,128)S(1)}, s32[4,12]{1,0:T(4,128)}, u32[]{:S(2)}) copy-start(s32[4,12]{1,0:T(4,128)} %off_ref.5) | copy-start | bytes 580
  70.5 24.6 %all-to-all-start.1 = ((f32[16,8,128]{2,1,0:T(8,128)}), f32[16,8,128]{2,1,0:T(8,128)S(1)}, u32[]{:S(2)}, u32[]{:S(2)}) async-start(f32[16,8,128]{2,1,0:T(8,128)} %broadcast_in_dim.5), calls=%async_computation.1 | async-start | bytes 131072 | tf_op jit(solution)/shard_map/all_to_all | solution.py:250

commit v2 on v1

--- a/solution.py
+++ b/solution.py
@@ -21,6 +21,7 @@
 N_NEAR = 4
 ROWS1, ROWS2, ROWS3 = 32, 8, 2
 NEG = -1e30
+CUTS = 4
 F32 = jnp.float32
 BF16 = jnp.bfloat16
 VMEM = pl.BlockSpec(memory_space=pltpu.VMEM)
@@ -55,8 +56,18 @@
     return jnp.concatenate([jnp.where(low, value, zero), jnp.where(low, zero, value)], 0)
 
 
-def pick_kernel(off_ref, k_ref, v_ref, q_ref, g_ref, near_ref, mid_ref, far_ref):
-    refs = (k_ref, v_ref, q_ref, g_ref)
+def pick_kernel(off_ref, k_hbm, v_hbm, q_hbm, g_hbm, near_ref, mid_ref, far_ref, refs, sems):
+    copies = []
+    for array, source in enumerate((k_hbm, v_hbm, q_hbm, g_hbm)):
+        for part in range(CUTS):
+            rows = pl.ds(part * (TOK // CUTS), TOK // CUTS)
+            copies.append(
+                pltpu.make_async_copy(
+                    source.at[rows], refs.at[array, rows], sems.at[array, part]
+                )
+            )
+    for copy in copies:
+        copy.start()
     row = iota((48, TOK), 0)
     tok = iota((48, TOK), 1)
     base = jnp.where(row < 32, row * 4, jnp.where(row < 40, (row - 32) * 16, (row % 2) * 64))
@@ -68,17 +79,27 @@
         live = (row < 40) | ((row - 40) // 2 == array)
         return jnp.where((tok == base + off) & live, 1.0, 0.0).astype(BF16)
 
+    far = [None] * PAIRS
+    for first in (0, 2):
+        for copy in copies[first * CUTS : (first + 2) * CUTS]:
+            copy.wait()
+        for pair in range(PAIRS):
+            picked = []
+            for array in (first, first + 1):
+                choose = jnp.concatenate(
+                    [selector(2 * pair, array), selector(2 * pair + 1, array)], 0
+                )
+                picked.append(halves(dot(choose, refs[array, :, lanes(pair)])))
+            near_ref[first * 32 : first * 32 + 64, lanes(pair)] = jnp.concatenate(
+                [x[:32] for x in picked], 0
+            ).astype(BF16)
+            mid_ref[first * 8 : first * 8 + 16, lanes(pair)] = jnp.concatenate(
+                [x[32:40] for x in picked], 0
+            ).astype(BF16)
+            both = picked[0][40:] + picked[1][40:]
+            far[pair] = both if far[pair] is None else far[pair] + both
     for pair in range(PAIRS):
-        picked = []
-        for array in range(4):
-            choose = jnp.concatenate(
-                [selector(2 * pair, array), selector(2 * pair + 1, array)], 0
-            )
-            picked.append(halves(dot(choose, refs[array][:, lanes(pair)])))
-        near_ref[:, lanes(pair)] = jnp.concatenate([x[:32] for x in picked], 0).astype(BF16)
-        mid_ref[:, lanes(pair)] = jnp.concatenate([x[32:40] for x in picked], 0).astype(BF16)
-        far = picked[0][40:] + picked[1][40:] + picked[2][40:] + picked[3][40:]
-        far_ref[:, lanes(pair)] = far.astype(BF16)
+        far_ref[:, lanes(pair)] = jnp.concatenate([far[pair]] * N_FAR, 0).astype(BF16)
 
 
 def split_kernel(far_ref, mid_ref, kv_ref, qg_ref):
@@ -104,39 +125,87 @@
     return jnp.concatenate([own_ref[:, cols]] + one + two + three, 0)
 
 
-def chosen(off_ref, head, level):
-    return (iota((TOK, 1), 0) & (GROUPS[level] - 1)) == off_ref[level, head]
+def chosen(off_ref, pair, level, tok):
+    half = tok.shape[0] // 2
+    off = jnp.where(
+        iota(tok.shape, 0) < half, off_ref[level, 2 * pair], off_ref[level, 2 * pair + 1]
+    )
+    return (tok & (GROUPS[level] - 1)) == off
+
+
+def softmax(scores, live):
+    blocks = [scores[:, level * 128 : level * 128 + 128] for level in range(4)]
+    for level in range(1, 4):
+        blocks[level] = jnp.where(live[level - 1], blocks[level], NEG)
+    top = jnp.maximum(jnp.maximum(blocks[0], blocks[1]), jnp.maximum(blocks[2], blocks[3]))
+    top = jnp.max(top, axis=1, keepdims=True)
+    raw = [jnp.exp(block - top) for block in blocks]
+    total = jnp.sum((raw[0] + raw[1]) + (raw[2] + raw[3]), axis=1, keepdims=True)
+    return jnp.concatenate(raw, 1), total, top
+
+
+def stat_kernel(
+    off_ref, k_ref, v_ref, near_ref, mid_ref, far_ref, near_rows_ref, back_ref, stat_ref
+):
+    row = iota((48, 1), 0)
+    both = iota((96, 128), 0)
+    slot = jnp.where(both < 48, both, both - 48)
+    sums = [None] * 8
+
+    def pick(level, pair):
+        return jnp.where(both < 48, off_ref[level, 2 * pair], off_ref[level, 2 * pair + 1])
+
+    for pair in range(PAIRS):
+        cols = lanes(pair)
+        far = far_ref[:16, cols].astype(F32)[:8]
+        mid = mid_ref[16:, cols].astype(F32)
+        near = near_ref[64:, cols].astype(F32)
+        query = jnp.concatenate([near[:32], mid[:8], pltpu.roll(far, 4, 0)], 0).astype(BF16)
+        grad = stacked(jnp.concatenate([near[32:], mid[8:], pltpu.roll(far, 2, 0)], 0))
+        keys = gathered(k_ref, near_rows_ref, back_ref, 0, pair)
+        values = gathered(v_ref, near_rows_ref, back_ref, 1, pair)
+        tok = jnp.where(
+            slot < 32,
+            slot * 4 + pick(1, pair),
+            jnp.where(slot < 40, (slot - 32) * 16 + pick(2, pair), slot % 2 * 64 + pick(3, pair)),
+        )
+        live = [chosen(off_ref, pair, level, tok) for level in range(1, 4)]
+        raw, total, top = softmax(dot_t(stacked(query), keys) * SCALE, live)
+        out = (dot(raw.astype(BF16), values) * (1.0 / total)).astype(BF16).astype(F32)
+        delta = jnp.sum(grad * out, axis=1, keepdims=True)
+        logs = top + jnp.log(total)
+        turn = pair // 2
+        lane = jnp.where(
+            row < 32,
+            row + 32 * turn,
+            jnp.where(
+                row < 40, row + 64 + 8 * turn, jnp.where(row < 42, row + 80 + 2 * turn, -1)
+            ),
+        )
+        hit = iota((48, 128), 1) == lane
+        for side in range(2):
+            for kind, column in enumerate((logs, delta)):
+                line = jnp.sum(
+                    jnp.where(hit, column[side * 48 : side * 48 + 48], 0.0), axis=0, keepdims=True
+                )
+                place = 2 * ((2 * pair + side) % 4) + kind
+                sums[place] = line if sums[place] is None else sums[place] + line
+    stat_ref[...] = jnp.concatenate(sums * N_FAR, 0)
 
 
 def forward_kernel(
-    off_ref, k_ref, v_ref, q_ref, g_ref, near_ref, back_ref, att_ref, gq_ref, stat_ref, own_ref
+    off_ref, k_ref, v_ref, q_ref, g_ref, near_ref, back_ref, att_ref, gq_ref, own_ref
 ):
-    tok = iota((TOK, 128), 0)
-    lane = iota((1, 128), 1)
-    eye = tok == iota((TOK, 128), 1)
-    sums = [None] * 8
+    eye = iota((TOK, 128), 0) == iota((TOK, 128), 1)
+    row = iota((2 * TOK, 128), 0)
     for pair in range(PAIRS):
         keys = gathered(k_ref, near_ref, back_ref, 0, pair)
         values = gathered(v_ref, near_ref, back_ref, 1, pair)
         grad = stacked(g_ref[:, lanes(pair)])
         scores = dot_t(stacked(q_ref[:, lanes(pair)]), keys) * SCALE
-        live = [
-            jnp.concatenate(
-                [chosen(off_ref, 2 * pair, level), chosen(off_ref, 2 * pair + 1, level)], 0
-            )
-            for level in range(1, 4)
-        ]
-        blocks = [scores[:, level * 128 : level * 128 + 128] for level in range(4)]
-        top = blocks[0]
-        for level in range(1, 4):
-            top = jnp.maximum(top, jnp.where(live[level - 1], blocks[level], NEG))
-        top = jnp.max(top, axis=1, keepdims=True)
-        raw = [jnp.exp(blocks[0] - top)]
-        for level in range(1, 4):
-            raw.append(jnp.exp(blocks[level] - jnp.where(live[level - 1], top, -NEG)))
-        total = jnp.sum(raw[0] + raw[1] + raw[2] + raw[3], axis=1, keepdims=True)
+        live = [chosen(off_ref, pair, level, row) for level in range(1, 4)]
+        raw, total, top = softmax(scores, live)
         inverse = 1.0 / total
-        raw = jnp.concatenate(raw, 1)
         out = halves(dot(raw.astype(BF16), values) * inverse).astype(BF16)
         att_ref[:, lanes(pair)] = out
         out = out.astype(F32)
@@ -147,31 +216,12 @@
         logs = top + jnp.log(total)
         for side in range(2):
             head = 2 * pair + side
-            turn = head // 4
-            one = lane - 32 * turn
-            two = lane - 96 - 8 * turn
-            three = lane - 120 - 2 * turn
-            source = jnp.where(
-                (one >= 0) & (one < 32),
-                one * 4 + off_ref[1, head],
-                jnp.where(
-                    (two >= 0) & (two < 8),
-                    two * 16 + off_ref[2, head],
-                    jnp.where(
-                        (three >= 0) & (three < 2), three * 64 + off_ref[3, head], -1
-                    ),
-                ),
-            )
-            hit = tok == source
             for kind, column in enumerate((logs, delta)):
-                column = column[side * TOK : side * TOK + TOK]
                 own_ref[2 * head + kind : 2 * head + kind + 1, :] = jnp.sum(
-                    jnp.where(eye, column, 0.0), axis=0, keepdims=True
+                    jnp.where(eye, column[side * TOK : side * TOK + TOK], 0.0),
+                    axis=0,
+                    keepdims=True,
                 )
-                line = jnp.sum(jnp.where(hit, column, 0.0), axis=0, keepdims=True)
-                place = 2 * (head % 4) + kind
-                sums[place] = line if sums[place] is None else sums[place] + line
-    stat_ref[...] = jnp.concatenate(sums, 0)
 
 
 def backward_kernel(
@@ -179,7 +229,9 @@
     gk_ref, gv_ref, line_ref,
 ):
     lane = iota((8, 128), 1)
+    row = iota((2 * TOK, 128), 0)
     mine = where_ref[0]
+    side = where_ref[1] * 2
 
     def block(d, peer):
         return stat_ref[pl.ds(pl.multiple_of((d * N_FAR + peer) * 8, 8), 8), :]
@@ -193,12 +245,13 @@
             moved = pltpu.roll(value, (at - start - width * turn) % 128, 1)
             acc[level][turn] = jnp.where(inside, moved, acc[level][turn])
 
-    for d in range(N_NEAR):
-        put(0, block(d, mine), d * 32, 32, 0)
+    for at in range(N_NEAR):
+        d = (at % 2 * 2) ^ side | at // 2
+        put(0, block(d, mine), at * 32, 32, 0)
         for slot, step in enumerate((0, 2, 1, 3)):
-            put(1, block(d, mine ^ step), d * 32 + slot * 8, 8, 96)
+            put(1, block(d, mine ^ step), at * 32 + slot * 8, 8, 96)
         for peer in range(N_FAR):
-            put(2, block(d, peer), d * 32 + peer * 2, 2, 120)
+            put(2, block(d, peer), at * 32 + peer * 2, 2, 120)
     for level in range(3):
         for turn in range(3):
             line_ref[turn * 8 : turn * 8 + 8, level * 128 : level * 128 + 128] = acc[level][turn]
@@ -208,6 +261,7 @@
         grads = gathered(g_ref, near_ref, back_ref, 3, pair)
         scores = dot_t(stacked(k_ref[:, lanes(pair)]), queries) * SCALE
         grad_probs = dot_t(stacked(v_ref[:, lanes(pair)]), grads)
+        live = [None] + [chosen(off_ref, pair, level, row) for level in range(1, 4)]
         probs, grad_scores = [], []
         for side in range(2):
             head = 2 * pair + side
@@ -224,7 +278,7 @@
                     delta_line = line_ref[2 * head + 1 : 2 * head + 2, at]
                 power = scores[rows, cols] - log_line
                 if level:
-                    power = jnp.where(chosen(off_ref, head, level), power, NEG)
+                    power = jnp.where(live[level][rows], power, NEG)
                 prob = jnp.exp(power)
                 probs_row.append(prob.astype(BF16))
                 grad_row.append((prob * (grad_probs[rows, cols] - delta_line)).astype(BF16))
@@ -245,35 +299,39 @@
 
 
 def to_far(value):
-    rows, cols = value.shape
-    spread = jnp.broadcast_to(value[None], (N_FAR, rows, cols)).reshape(N_FAR * rows, cols)
-    return lax.all_to_all(spread, FAR, 0, 0, tiled=True)
+    return lax.all_to_all(value, FAR, 0, 0, tiled=True)
 
 
 def to_near(value):
     return lax.all_gather(value, NEAR, axis=0, tiled=True)
 
 
+def to_pair(value):
+    other = lax.ppermute(value, "zl", [(0, 1), (1, 0)])
+    return lax.all_gather(jnp.concatenate([value, other], 0), "c", axis=0, tiled=True)
+
+
 def swap_mid(value, step):
     return lax.ppermute(value, "zm", [(i, i ^ step) for i in range(4)])
 
 
 def on_device(queries, key_states, value_states, grad_output, head_offsets):
     mine = (lax.axis_index("yh") * 2 + lax.axis_index("zh")) * 4 + lax.axis_index("zm")
+    place = jnp.stack([mine, lax.axis_index("zl")])
     own = (key_states, value_states, queries, grad_output)
     near, mid, far = pl.pallas_call(
         pick_kernel,
         name="pick",
-        out_shape=(shape(128, FULL), shape(32, FULL), shape(8, FULL)),
-        in_specs=[SMEM] + [VMEM] * 4,
+        out_shape=(shape(128, FULL), shape(32, FULL), shape(8 * N_FAR, FULL)),
+        in_specs=[SMEM] + [pl.BlockSpec(memory_space=pl.ANY)] * 4,
         out_specs=(VMEM,) * 3,
-        compiler_params=PARAMS,
+        scratch_shapes=[pltpu.VMEM((4, TOK, FULL), BF16), pltpu.SemaphoreType.DMA((4, CUTS))],
+        compiler_params=pltpu.CompilerParams(vmem_limit_bytes=62 * 1024 * 1024),
         cost_estimate=cost(200_000_000, 1_100_000),
     )(head_offsets, *own)
     far_rows = to_far(far)
-    mid_rows = jnp.concatenate([mid, swap_mid(mid, 2)], 0)
-    mid_rows = jnp.concatenate([mid_rows, swap_mid(mid_rows, 1)], 0)
-    near_rows = to_near(near)
+    mid_rows = jnp.concatenate([mid, swap_mid(mid, 2), swap_mid(mid, 1), swap_mid(mid, 3)], 0)
+    near_rows = to_pair(near)
     kv_rows, qg_rows = pl.pallas_call(
         split_kernel,
         name="split",
@@ -283,23 +341,31 @@
         compiler_params=PARAMS,
         cost_estimate=cost(100_000_000, 800_000),
     )(far_rows, mid_rows)
-    kv_rows = to_near(kv_rows)
-    attended, grad_query, stats, own_stats = pl.pallas_call(
+    kv_rows = to_pair(kv_rows)
+    stats = pl.pallas_call(
+        stat_kernel,
+        name="stats",
+        out_shape=shape(8 * N_FAR, 128, dtype=F32),
+        in_specs=[SMEM] + [VMEM] * 7,
+        out_specs=VMEM,
+        compiler_params=PARAMS,
+        cost_estimate=cost(200_000_000, 2_000_000, 300_000),
+    )(head_offsets, key_states, value_states, near, mid, far, near_rows, kv_rows)
+    attended, grad_query, own_stats = pl.pallas_call(
         forward_kernel,
         name="forward",
         out_shape=(
             shape(TOK, FULL),
             shape(TOK, FULL),
-            shape(8, 128, dtype=F32),
             shape(2 * HEADS, 128, dtype=F32),
         ),
         in_specs=[SMEM] + [VMEM] * 6,
-        out_specs=(VMEM,) * 4,
+        out_specs=(VMEM,) * 3,
         compiler_params=PARAMS,
         cost_estimate=cost(1_000_000_000, 3_000_000, 800_000),
     )(head_offsets, *own, near_rows, kv_rows)
     all_stats = to_near(to_far(stats))
-    qg_rows = to_near(qg_rows)
+    qg_rows = to_pair(qg_rows)
     grad_key, grad_value = pl.pallas_call(
         backward_kernel,
         name="backward",
@@ -309,7 +375,7 @@
         scratch_shapes=[pltpu.VMEM((2 * HEADS, 3 * 128), F32)],
         compiler_params=PARAMS,
         cost_estimate=cost(1_000_000_000, 3_000_000, 800_000),
-    )(head_offsets, mine.reshape(1), *own, near_rows, qg_rows, own_stats, all_stats)
+    )(head_offsets, place, *own, near_rows, qg_rows, own_stats, all_stats)
     return attended, grad_query, grad_key, grad_value
 
 

time: 106 us -> 98.1 us (0.925)
  blocking collectives: 37.6 us -> 18.1 us
  starting transfers between devices: 38.2 us -> 51.4 us
  local copies, waits for them, and re-layouts: 5.74 us -> 1 us
  Pallas kernels: 10.1 us -> 14.8 us
  waiting for transfers between devices: 13.2 us -> 11.2 us
    all_gather x4 -> x1, blocking collectives: 37.6 us -> 7.4 us  [to_near(): return lax.all_gather(value, NEAR, axis=0, tiled=True)]
    all_gather x0 -> x3, blocking collectives: none -> 10.7 us  [to_pair(): lax.all_gather(jnp.concatenate([value, other], 0), 'c', axis=0, tiled=True)]
    ppermute x0 -> x3, starting transfers between devices: none -> 7.86 us  [to_pair(): other = lax.ppermute(value, 'zl', [(0, 1), (1, 0)])]
    ppermute x2 -> x3, waiting for transfers between devices: 10 us -> 5.93 us  [swap_mid(): return lax.ppermute(value, 'zm', [(i, i ^ step) for i in range(4)])]
    ppermute x2 -> x3, starting transfers between devices: 9.14 us -> 13.2 us  [swap_mid(): return lax.ppermute(value, 'zm', [(i, i ^ step) for i in range(4)])]
    unnamed x20 -> x16, local copies, waits for them, and re-layouts: 4.41 us -> 1 us
    pallas_call x0 -> x1, Pallas kernels: none -> 3.15 us  [on_device(): pl.pallas_call(stat_kernel, name='stats', out_shape=shape(8 * N_FAR, 128,...]
    pallas_call x1, Pallas kernels: 0.91 us -> 3.06 us  [on_device(): pl.pallas_call(pick_kernel, name='pick', out_shape=(shape(128, FULL), sha...]
  transfers between devices with their start and end apart: 4 -> 8, of which waited for: 2 -> 3; matrix products, arithmetic and copies ran while one was open for 0% -> 0% of each run, Pallas kernels for 0% -> 8%
where the time goes in v2:
time: 98.1 us; the launch traced here: 97.6 us
  starting transfers between devices  51.4 us (52%)
  blocking collectives  18.1 us (18%)
  Pallas kernels  14.8 us (15%)
  waiting for transfers between devices  11.2 us (11%)
  local copies, waits for them, and re-layouts  1 us (1%)
    all_to_all x2, starting transfers between devices, to_far(): return lax.all_to_all(value, FAR, 0, 0, tiled=True)  30.4 us
    ppermute x3, starting transfers between devices, swap_mid(): return lax.ppermute(value, 'zm', [(i, i ^ step) for i in range(4)])  13.2 us
    all_gather x3, blocking collectives, to_pair(): lax.all_gather(jnp.concatenate([value, other], 0), 'c', axis=0, tiled=True)  10.7 us
    ppermute x3, starting transfers between devices, to_pair(): other = lax.ppermute(value, 'zl', [(0, 1), (1, 0)])  7.86 us
    all_gather x1, blocking collectives, to_near(): return lax.all_gather(value, NEAR, axis=0, tiled=True)  7.4 us
    ppermute x3, waiting for transfers between devices, swap_mid(): return lax.ppermute(value, 'zm', [(i, i ^ step) for i in range(4)])  5.93 us
    all_to_all x2, waiting for transfers between devices, to_far(): return lax.all_to_all(value, FAR, 0, 0, tiled=True)  5.26 us
    pallas_call x1, Pallas kernels, on_device(): pl.pallas_call(forward_kernel, name='forward', out_shape=(shape(TOK, FULL...  4.85 us
  transfers between devices with their start and end apart: 8, of which 3 were waited for; matrix products, arithmetic and copies ran while one was open for 0% of the time, Pallas kernels for 8%

profile of v2, /device:TPU:1, one launch (start us, length us, event | category | flops | bytes accessed | tf_op | source)
XLA Modules:
  0.0 97.6 jit_solution(14529146132549218665)
XLA Ops:
  0.6 3.1 %pick.1 = (bf16[128,768]{1,0:T(8,128)(2,1)}, bf16[32,768]{1,0:T(8,128)(2,1)}, bf16[128,768]{1,0:T(8,128)(2,1)}) custom-call(s32[4,12]{1,0:T(4,128)} %off_ref.7, bf16[128,768]{1,0:T(8,128)(2,1)} %k_ref.5, bf16[128,768]{1,0:T(8,128)(2,1)} %v_ref.5, bf16[128,768]{1,0:T(8,128)(2,1)} %q_ref.3, bf16[128,768]{1,0:T(8,128)(2,1)} %g_ref.3), custom_call_target="tpu_custom_call" | custom-call | flops 200000000 | bytes 1100000 | tf_op jit(solution)/shard_map/pick/pallas_call | solution.py:322
  3.7 18.5 %all-to-all-start = ((bf16[16,8,768]{2,1,0:T(8,128)(2,1)}), bf16[16,8,768]{2,1,0:T(8,128)(2,1)S(1)}, u32[]{:S(2)}, u32[]{:S(2)}) async-start(bf16[16,8,768]{2,1,0:T(8,128)(2,1)} %bitcast.6), calls=%async_computation | async-start | bytes 393216 | tf_op jit(solution)/shard_map/all_to_all | solution.py:302
  22.3 7.2 %collective-permute-start.1 = (bf16[32,768]{1,0:T(8,128)(2,1)S(1)}, bf16[32,768]{1,0:T(8,128)(2,1)S(1)}, u32[]{:S(2)}, u32[]{:S(2)}) collective-permute-start(bf16[32,768]{1,0:T(8,128)(2,1)S(1)} %copy-done.6), channel_id=1, source_target_pairs={{0,64},{32,96},{64,0},{96,32},{1,65},{33,97},{65,1},{97,33},{2,66}... | collective-permute-start | bytes 147464 | tf_op jit(solution)/shard_map/ppermute | solution.py:315
  29.4 4.0 %collective-permute-start.2 = (bf16[32,768]{1,0:T(8,128)(2,1)S(1)}, bf16[32,768]{1,0:T(8,128)(2,1)S(1)}, u32[]{:S(2)}, u32[]{:S(2)}) collective-permute-start(bf16[32,768]{1,0:T(8,128)(2,1)S(1)} %copy-done.6), channel_id=1, source_target_pairs={{0,32},{32,0},{64,96},{96,64},{1,33},{33,1},{65,97},{97,65},{2,34}... | collective-permute-start | bytes 147464 | tf_op jit(solution)/shard_map/ppermute | solution.py:315
  33.4 2.0 %collective-permute-start.3 = (bf16[32,768]{1,0:T(8,128)(2,1)S(1)}, bf16[32,768]{1,0:T(8,128)(2,1)S(1)}, u32[]{:S(2)}, u32[]{:S(2)}) collective-permute-start(bf16[32,768]{1,0:T(8,128)(2,1)S(1)} %copy-done.6), channel_id=1, source_target_pairs={{0,96},{32,64},{64,32},{96,0},{1,97},{33,65},{65,33},{97,1},{2,98}... | collective-permute-start | bytes 147464 | tf_op jit(solution)/shard_map/ppermute | solution.py:315
  35.5 2.6 %collective-permute-start = (bf16[128,768]{1,0:T(8,128)(2,1)S(1)}, bf16[128,768]{1,0:T(8,128)(2,1)S(1)}, u32[]{:S(2)}, u32[]{:S(2)}) collective-permute-start(bf16[128,768]{1,0:T(8,128)(2,1)S(1)} %copy-done.3), channel_id=1, source_target_pairs={{0,16},{16,0},{1,17},{17,1},{2,18},{18,2},{3,19},{19,3},{4,20},{20... | collective-permute-start | bytes 589832 | tf_op jit(solution)/shard_map/ppermute | solution.py:310
  38.1 0.1 pad_add_fusion.where_ref
  38.2 1.3 %collective-permute-done.1 = bf16[32,768]{1,0:T(8,128)(2,1)S(1)} collective-permute-done((bf16[32,768]{1,0:T(8,128)(2,1)S(1)}, bf16[32,768]{1,0:T(8,128)(2,1)S(1)}, u32[]{:S(2)}, u32[]{:S(2)}) %collective-permute-start.1) | collective-permute-done | bytes 49184 | tf_op jit(solution)/shard_map/ppermute | solution.py:315
  39.5 4.6 %collective-permute-done.3 = bf16[32,768]{1,0:T(8,128)(2,1)S(1)} collective-permute-done((bf16[32,768]{1,0:T(8,128)(2,1)S(1)}, bf16[32,768]{1,0:T(8,128)(2,1)S(1)}, u32[]{:S(2)}, u32[]{:S(2)}) %collective-permute-start.3) | collective-permute-done | bytes 49184 | tf_op jit(solution)/shard_map/ppermute | solution.py:315
  44.2 0.3 split.1
  44.5 2.7 %collective-permute-start.4 = (bf16[128,768]{1,0:T(8,128)(2,1)S(1)}, bf16[128,768]{1,0:T(8,128)(2,1)S(1)}, u32[]{:S(2)}, u32[]{:S(2)}) collective-permute-start(bf16[128,768]{1,0:T(8,128)(2,1)S(1)} %get-tuple-element.17), channel_id=1, source_target_pairs={{0,16},{16,0},{1,17},{17,1},{2,18},{18,2},{3,19},{19,3},{4,20},{20... | collective-permute-start | bytes 589832 | tf_op jit(solution)/shard_map/ppermute | solution.py:310
  47.2 5.3 %all_gather.12.near_ref.near_rows_ref = bf16[512,768]{1,0:T(8,128)(2,1)S(1)} all-gather(bf16[256,768]{1,0:T(8,128)(2,1)S(1)} %pad_maximum_fusion), channel_id=1, replica_groups=mesh['yh'=2,'zh'=2,'zm'=4,'zl'=2,'c'=2,'dp'=8] {'c'}, dimensions={0}, use_global_device_ids=true | all-gather | bytes 1179648 | tf_op jit(solution)/shard_map/all_gather | solution.py:311
  52.5 2.5 %collective-permute-start.5 = (bf16[128,768]{1,0:T(8,128)(2,1)S(1)}, bf16[128,768]{1,0:T(8,128)(2,1)S(1)}, u32[]{:S(2)}, u32[]{:S(2)}) collective-permute-start(bf16[128,768]{1,0:T(8,128)(2,1)S(1)} %get-tuple-element.20), channel_id=1, source_target_pairs={{0,16},{16,0},{1,17},{17,1},{2,18},{18,2},{3,19},{19,3},{4,20},{20... | collective-permute-start | bytes 589832 | tf_op jit(solution)/shard_map/ppermute | solution.py:310
  55.1 0.0 copy-start
  55.1 2.8 %all_gather.13.back_ref = bf16[512,768]{1,0:T(8,128)(2,1)S(1)} all-gather(bf16[256,768]{1,0:T(8,128)(2,1)S(1)} %pad_maximum_fusion.1), channel_id=1, replica_groups=mesh['yh'=2,'zh'=2,'zm'=4,'zl'=2,'c'=2,'dp'=8] {'c'}, dimensions={0}, use_global_device_ids=true | all-gather | bytes 1179648 | tf_op jit(solution)/shard_map/all_gather | solution.py:311
  57.9 3.2 %stats.1 = f32[128,128]{1,0:T(8,128)} custom-call(s32[4,12]{1,0:T(4,128)S(1)} %copy-done.7, bf16[128,768]{1,0:T(8,128)(2,1)S(1)} %copy-done.1, bf16[128,768]{1,0:T(8,128)(2,1)S(1)} %copy-done.2, bf16[128,768]{1,0:T(8,128)(2,1)S(1)} %copy-done.3, bf16[32,768]{1,0:T(8,128)(2,1)S(1)} %copy-done.6, bf16[128,768]{1,0:T(8,128)(2,1)S(1)} %copy-done, ...), custom_call_target="tpu_custom_call" | custom-call | flops 200000000 | bytes 2000000 | tf_op jit(solution)/shard_map/stats/pallas_call | solution.py:345
  61.1 11.8 %all-to-all-start.1 = ((f32[16,8,128]{2,1,0:T(8,128)}), f32[16,8,128]{2,1,0:T(8,128)S(1)}, u32[]{:S(2)}, u32[]{:S(2)}) async-start(f32[16,8,128]{2,1,0:T(8,128)} %bitcast.4), calls=%async_computation.1 | async-start | bytes 131072 | tf_op jit(solution)/shard_map/all_to_all | solution.py:302
  73.0 0.9 copy-done.4
  73.8 0.1 copy-done.5
  73.9 4.9 %forward.1 = (bf16[128,768]{1,0:T(8,128)(2,1)}, bf16[128,768]{1,0:T(8,128)(2,1)}, f32[24,128]{1,0:T(8,128)S(1)}) custom-call(s32[4,12]{1,0:T(4,128)S(1)} %copy-done.7, bf16[128,768]{1,0:T(8,128)(2,1)S(1)} %copy-done.1, bf16[128,768]{1,0:T(8,128)(2,1)S(1)} %copy-done.2, bf16[128,768]{1,0:T(8,128)(2,1)S(1)} %copy-done.4, bf16[128,768]{1,0:T(8,128)(2,1)S(1)} %copy-done.5, ...), custom_call_target="tpu_custom_call" | custom-call | flops 1000000000 | bytes 3000000 | tf_op jit(solution)/shard_map/forward/pallas_call | solution.py:354
  78.8 2.6 %all_gather.14.back_ref = bf16[512,768]{1,0:T(8,128)(2,1)S(1)} all-gather(bf16[256,768]{1,0:T(8,128)(2,1)S(1)} %pad_maximum_fusion.2), channel_id=1, replica_groups=mesh['yh'=2,'zh'=2,'zm'=4,'zl'=2,'c'=2,'dp'=8] {'c'}, dimensions={0}, use_global_device_ids=true | all-gather | bytes 1179648 | tf_op jit(solution)/shard_map/all_gather | solution.py:311
  81.4 5.3 %all-to-all-done.1 = f32[16,8,128]{2,1,0:T(8,128)S(1)} async-done(((f32[16,8,128]{2,1,0:T(8,128)}), f32[16,8,128]{2,1,0:T(8,128)S(1)}, u32[]{:S(2)}, u32[]{:S(2)}) %all-to-all-start.1) | async-done | bytes 65568 | tf_op jit(solution)/shard_map/all_to_all | solution.py:302
  86.7 7.4 %all_gather.15.stat_ref = f32[512,128]{1,0:T(8,128)S(1)} all-gather(f32[128,128]{1,0:T(8,128)S(1)} %bitcast.8), channel_id=1, replica_groups=mesh['yh'=2,'zh'=2,'zm'=4,'zl'=2,'c'=2,'dp'=8] {'zl','c'}, dimensions={0}, use_global_device_ids=true | all-gather | bytes 327680 | tf_op jit(solution)/shard_map/all_gather | solution.py:306
  94.1 3.5 %backward.1 = (bf16[128,768]{1,0:T(8,128)(2,1)}, bf16[128,768]{1,0:T(8,128)(2,1)}) custom-call(s32[4,12]{1,0:T(4,128)S(1)} %copy-done.7, s32[2]{0:T(128)S(1)} %pad_add_fusion.where_ref, bf16[128,768]{1,0:T(8,128)(2,1)S(1)} %copy-done.1, bf16[128,768]{1,0:T(8,128)(2,1)S(1)} %copy-done.2, bf16[128,768]{1,0:T(8,128)(2,1)S(1)} %copy-done.4, ...), custom_call_target="tpu_custom_call" | custom-call | flops 1000000000 | bytes 3000000 | tf_op jit(solution)/shard_map/backward/pallas_call | solution.py:369
  (22 shorter events, 0.2 us)
Async XLA Ops:
  3.7 18.6 %copy-start.6 = (bf16[32,768]{1,0:T(8,128)(2,1)S(1)}, bf16[32,768]{1,0:T(8,128)(2,1)}, u32[]{:S(2)}) copy-start(bf16[32,768]{1,0:T(8,128)(2,1)} %get-tuple-element.16.mid_ref) | copy-start | bytes 147460
  3.7 31.8 %copy-start.3 = (bf16[128,768]{1,0:T(8,128)(2,1)S(1)}, bf16[128,768]{1,0:T(8,128)(2,1)}, u32[]{:S(2)}) copy-start(bf16[128,768]{1,0:T(8,128)(2,1)} %get-tuple-element.14.near_ref) | copy-start | bytes 589828
  3.7 40.5 %all-to-all-start = ((bf16[16,8,768]{2,1,0:T(8,128)(2,1)}), bf16[16,8,768]{2,1,0:T(8,128)(2,1)S(1)}, u32[]{:S(2)}, u32[]{:S(2)}) async-start(bf16[16,8,768]{2,1,0:T(8,128)(2,1)} %bitcast.6), calls=%async_computation | async-start | bytes 393216 | tf_op jit(solution)/shard_map/all_to_all | solution.py:302
  22.3 17.3 %collective-permute-start.1 = (bf16[32,768]{1,0:T(8,128)(2,1)S(1)}, bf16[32,768]{1,0:T(8,128)(2,1)S(1)}, u32[]{:S(2)}, u32[]{:S(2)}) collective-permute-start(bf16[32,768]{1,0:T(8,128)(2,1)S(1)} %copy-done.6), channel_id=1, source_target_pairs={{0,64},{32,96},{64,0},{96,32},{1,65},{33,97},{65,1},{97,33},{2,66}... | collective-permute-start | bytes 147464 | tf_op jit(solution)/shard_map/ppermute | solution.py:315
  29.4 10.1 %collective-permute-start.2 = (bf16[32,768]{1,0:T(8,128)(2,1)S(1)}, bf16[32,768]{1,0:T(8,128)(2,1)S(1)}, u32[]{:S(2)}, u32[]{:S(2)}) collective-permute-start(bf16[32,768]{1,0:T(8,128)(2,1)S(1)} %copy-done.6), channel_id=1, source_target_pairs={{0,32},{32,0},{64,96},{96,64},{1,33},{33,1},{65,97},{97,65},{2,34}... | collective-permute-start | bytes 147464 | tf_op jit(solution)/shard_map/ppermute | solution.py:315
  33.4 10.7 %collective-permute-start.3 = (bf16[32,768]{1,0:T(8,128)(2,1)S(1)}, bf16[32,768]{1,0:T(8,128)(2,1)S(1)}, u32[]{:S(2)}, u32[]{:S(2)}) collective-permute-start(bf16[32,768]{1,0:T(8,128)(2,1)S(1)} %copy-done.6), channel_id=1, source_target_pairs={{0,96},{32,64},{64,32},{96,0},{1,97},{33,65},{65,33},{97,1},{2,98}... | collective-permute-start | bytes 147464 | tf_op jit(solution)/shard_map/ppermute | solution.py:315
  35.5 8.7 %collective-permute-start = (bf16[128,768]{1,0:T(8,128)(2,1)S(1)}, bf16[128,768]{1,0:T(8,128)(2,1)S(1)}, u32[]{:S(2)}, u32[]{:S(2)}) collective-permute-start(bf16[128,768]{1,0:T(8,128)(2,1)S(1)} %copy-done.3), channel_id=1, source_target_pairs={{0,16},{16,0},{1,17},{17,1},{2,18},{18,2},{3,19},{19,3},{4,20},{20... | collective-permute-start | bytes 589832 | tf_op jit(solution)/shard_map/ppermute | solution.py:310
  44.5 10.5 %collective-permute-start.4 = (bf16[128,768]{1,0:T(8,128)(2,1)S(1)}, bf16[128,768]{1,0:T(8,128)(2,1)S(1)}, u32[]{:S(2)}, u32[]{:S(2)}) collective-permute-start(bf16[128,768]{1,0:T(8,128)(2,1)S(1)} %get-tuple-element.17), channel_id=1, source_target_pairs={{0,16},{16,0},{1,17},{17,1},{2,18},{18,2},{3,19},{19,3},{4,20},{20... | collective-permute-start | bytes 589832 | tf_op jit(solution)/shard_map/ppermute | solution.py:310
  52.5 20.5 %collective-permute-start.5 = (bf16[128,768]{1,0:T(8,128)(2,1)S(1)}, bf16[128,768]{1,0:T(8,128)(2,1)S(1)}, u32[]{:S(2)}, u32[]{:S(2)}) collective-permute-start(bf16[128,768]{1,0:T(8,128)(2,1)S(1)} %get-tuple-element.20), channel_id=1, source_target_pairs={{0,16},{16,0},{1,17},{17,1},{2,18},{18,2},{3,19},{19,3},{4,20},{20... | collective-permute-start | bytes 589832 | tf_op jit(solution)/shard_map/ppermute | solution.py:310
  55.1 2.8 %copy-start = (bf16[128,768]{1,0:T(8,128)(2,1)S(1)}, bf16[128,768]{1,0:T(8,128)(2,1)}, u32[]{:S(2)}) copy-start(bf16[128,768]{1,0:T(8,128)(2,1)} %get-tuple-element.15.far_ref) | copy-start | bytes 589828
  55.1 2.8 %copy-start.1 = (bf16[128,768]{1,0:T(8,128)(2,1)S(1)}, bf16[128,768]{1,0:T(8,128)(2,1)}, u32[]{:S(2)}) copy-start(bf16[128,768]{1,0:T(8,128)(2,1)} %k_ref.5) | copy-start | bytes 589828
  55.1 2.8 %copy-start.2 = (bf16[128,768]{1,0:T(8,128)(2,1)S(1)}, bf16[128,768]{1,0:T(8,128)(2,1)}, u32[]{:S(2)}) copy-start(bf16[128,768]{1,0:T(8,128)(2,1)} %v_ref.5) | copy-start | bytes 589828
  55.1 2.8 %copy-start.7 = (s32[4,12]{1,0:T(4,128)S(1)}, s32[4,12]{1,0:T(4,128)}, u32[]{:S(2)}) copy-start(s32[4,12]{1,0:T(4,128)} %off_ref.7) | copy-start | bytes 580
  61.1 25.6 %all-to-all-start.1 = ((f32[16,8,128]{2,1,0:T(8,128)}), f32[16,8,128]{2,1,0:T(8,128)S(1)}, u32[]{:S(2)}, u32[]{:S(2)}) async-start(f32[16,8,128]{2,1,0:T(8,128)} %bitcast.4), calls=%async_computation.1 | async-start | bytes 131072 | tf_op jit(solution)/shard_map/all_to_all | solution.py:302
  72.9 0.9 copy-start.4
  72.9 1.0 %copy-start.5 = (bf16[128,768]{1,0:T(8,128)(2,1)S(1)}, bf16[128,768]{1,0:T(8,128)(2,1)}, u32[]{:S(2)}) copy-start(bf16[128,768]{1,0:T(8,128)(2,1)} %g_ref.3) | copy-start | bytes 589828

commit v3 on v2

--- a/solution.py
+++ b/solution.py
@@ -22,6 +22,7 @@
 ROWS1, ROWS2, ROWS3 = 32, 8, 2
 NEG = -1e30
 CUTS = 4
+ROOT_ROWS, ROOT_STATS = 13, 2
 F32 = jnp.float32
 BF16 = jnp.bfloat16
 VMEM = pl.BlockSpec(memory_space=pltpu.VMEM)
@@ -102,7 +103,8 @@
         far_ref[:, lanes(pair)] = jnp.concatenate([far[pair]] * N_FAR, 0).astype(BF16)
 
 
-def split_kernel(far_ref, mid_ref, kv_ref, qg_ref):
+def split_kernel(far_ref, mid_ref, q_ref, g_ref, kv_ref, qg_ref):
+    del q_ref, g_ref
     both = jnp.concatenate([far_ref[...], mid_ref[...]], 0)
     row = iota((128, 256), 0)
     col = iota((128, 256), 1)
@@ -234,7 +236,7 @@
     side = where_ref[1] * 2
 
     def block(d, peer):
-        return stat_ref[pl.ds(pl.multiple_of((d * N_FAR + peer) * 8, 8), 8), :]
+        return stat_ref[pl.ds(pl.multiple_of((d * N_FAR + (peer ^ ROOT_STATS)) * 8, 8), 8), :]
 
     zero = jnp.zeros((8, 128), F32)
     acc = [[zero] * 3 for _ in range(3)]
@@ -251,7 +253,7 @@
         for slot, step in enumerate((0, 2, 1, 3)):
             put(1, block(d, mine ^ step), at * 32 + slot * 8, 8, 96)
         for peer in range(N_FAR):
-            put(2, block(d, peer), at * 32 + peer * 2, 2, 120)
+            put(2, block(d, peer ^ ROOT_ROWS), at * 32 + peer * 2, 2, 120)
     for level in range(3):
         for turn in range(3):
             line_ref[turn * 8 : turn * 8 + 8, level * 128 : level * 128 + 128] = acc[level][turn]
@@ -298,8 +300,9 @@
     return pl.CostEstimate(flops=flops, bytes_accessed=moved, transcendentals=exps)
 
 
-def to_far(value):
-    return lax.all_to_all(value, FAR, 0, 0, tiled=True)
+def to_far(value, root):
+    order = [[peer ^ root for peer in range(N_FAR)]]
+    return lax.all_to_all(value, FAR, 0, 0, tiled=True, axis_index_groups=order)
 
 
 def to_near(value):
@@ -329,18 +332,18 @@
         compiler_params=pltpu.CompilerParams(vmem_limit_bytes=62 * 1024 * 1024),
         cost_estimate=cost(200_000_000, 1_100_000),
     )(head_offsets, *own)
-    far_rows = to_far(far)
+    far_rows = to_far(far, ROOT_ROWS)
     mid_rows = jnp.concatenate([mid, swap_mid(mid, 2), swap_mid(mid, 1), swap_mid(mid, 3)], 0)
     near_rows = to_pair(near)
     kv_rows, qg_rows = pl.pallas_call(
         split_kernel,
         name="split",
         out_shape=(shape(128, FULL), shape(128, FULL)),
-        in_specs=[VMEM] * 2,
+        in_specs=[VMEM] * 4,
         out_specs=(VMEM,) * 2,
         compiler_params=PARAMS,
         cost_estimate=cost(100_000_000, 800_000),
-    )(far_rows, mid_rows)
+    )(far_rows, mid_rows, queries, grad_output)
     kv_rows = to_pair(kv_rows)
     stats = pl.pallas_call(
         stat_kernel,
@@ -364,7 +367,7 @@
         compiler_params=PARAMS,
         cost_estimate=cost(1_000_000_000, 3_000_000, 800_000),
     )(head_offsets, *own, near_rows, kv_rows)
-    all_stats = to_near(to_far(stats))
+    all_stats = to_near(to_far(stats, ROOT_STATS))
     qg_rows = to_pair(qg_rows)
     grad_key, grad_value = pl.pallas_call(
         backward_kernel,

time: 98.1 us -> 88.9 us (0.906)
  starting transfers between devices: 51.4 us -> 47.1 us
  waiting for transfers between devices: 11.2 us -> 7.25 us
    ppermute x3, waiting for transfers between devices: 5.93 us -> 0.79 us  [swap_mid(): return lax.ppermute(value, 'zm', [(i, i ^ step) for i in range(4)])]
    ppermute x3, waiting for transfers between devices: 0.01 us -> 4.03 us  [to_pair(): other = lax.ppermute(value, 'zl', [(0, 1), (1, 0)])]
    all_to_all x2, starting transfers between devices: 30.4 us -> 26.5 us  [to_far(): return lax.all_to_all(value, FAR, 0, 0, tiled=True, axis_index_groups=order)]
    all_to_all x2, waiting for transfers between devices: 5.26 us -> 2.42 us  [to_far(): return lax.all_to_all(value, FAR, 0, 0, tiled=True, axis_index_groups=order)]
  transfers between devices with their start and end apart: 8 -> 8, of which waited for: 3 -> 3; matrix products, arithmetic and copies ran while one was open for 0% -> 0% of each run, Pallas kernels for 8% -> 9%
where the time goes in v3:
time: 88.9 us; the launch traced here: 88.4 us
  starting transfers between devices  47.1 us (53%)
  blocking collectives  18.2 us (20%)
  Pallas kernels  14.8 us (17%)
  waiting for transfers between devices  7.25 us (8%)
    all_to_all x2, starting transfers between devices, to_far(): return lax.all_to_all(value, FAR, 0, 0, tiled=True, axis_index_groups=order)  26.5 us
    ppermute x3, starting transfers between devices, swap_mid(): return lax.ppermute(value, 'zm', [(i, i ^ step) for i in range(4)])  13.2 us
    all_gather x3, blocking collectives, to_pair(): lax.all_gather(jnp.concatenate([value, other], 0), 'c', axis=0, tiled=True)  10.6 us
    all_gather x1, blocking collectives, to_near(): return lax.all_gather(value, NEAR, axis=0, tiled=True)  7.53 us
    ppermute x3, starting transfers between devices, to_pair(): other = lax.ppermute(value, 'zl', [(0, 1), (1, 0)])  7.46 us
    pallas_call x1, Pallas kernels, on_device(): pl.pallas_call(forward_kernel, name='forward', out_shape=(shape(TOK, FULL...  4.86 us
    ppermute x3, waiting for transfers between devices, to_pair(): other = lax.ppermute(value, 'zl', [(0, 1), (1, 0)])  4.03 us
    pallas_call x1, Pallas kernels, on_device(): pl.pallas_call(backward_kernel, name='backward', out_shape=(shape(TOK, FU...  3.47 us
  transfers between devices with their start and end apart: 8, of which 3 were waited for; matrix products, arithmetic and copies ran while one was open for 0% of the time, Pallas kernels for 9%

profile of v3, /device:TPU:1, one launch (start us, length us, event | category | flops | bytes accessed | tf_op | source)
XLA Modules:
  0.0 88.4 jit_solution(8451609719841455508)
XLA Ops:
  0.6 3.1 %pick.1 = (bf16[128,768]{1,0:T(8,128)(2,1)}, bf16[32,768]{1,0:T(8,128)(2,1)}, bf16[128,768]{1,0:T(8,128)(2,1)}) custom-call(s32[4,12]{1,0:T(4,128)} %off_ref.7, bf16[128,768]{1,0:T(8,128)(2,1)} %k_ref.5, bf16[128,768]{1,0:T(8,128)(2,1)} %v_ref.5, bf16[128,768]{1,0:T(8,128)(2,1)} %q_ref.5, bf16[128,768]{1,0:T(8,128)(2,1)} %g_ref.5), custom_call_target="tpu_custom_call" | custom-call | flops 200000000 | bytes 1100000 | tf_op jit(solution)/shard_map/pick/pallas_call | solution.py:325
  3.7 19.6 %all-to-all-start = ((bf16[16,8,768]{2,1,0:T(8,128)(2,1)}), bf16[16,8,768]{2,1,0:T(8,128)(2,1)S(1)}, u32[]{:S(2)}, u32[]{:S(2)}) async-start(bf16[16,8,768]{2,1,0:T(8,128)(2,1)} %bitcast.6), calls=%async_computation | async-start | bytes 393216 | tf_op jit(solution)/shard_map/all_to_all | solution.py:305
  23.4 4.0 %collective-permute-start.1 = (bf16[32,768]{1,0:T(8,128)(2,1)S(1)}, bf16[32,768]{1,0:T(8,128)(2,1)S(1)}, u32[]{:S(2)}, u32[]{:S(2)}) collective-permute-start(bf16[32,768]{1,0:T(8,128)(2,1)S(1)} %copy-done.6), channel_id=1, source_target_pairs={{0,64},{32,96},{64,0},{96,32},{1,65},{33,97},{65,1},{97,33},{2,66}... | collective-permute-start | bytes 147464 | tf_op jit(solution)/shard_map/ppermute | solution.py:318
  27.4 2.2 %collective-permute-start.2 = (bf16[32,768]{1,0:T(8,128)(2,1)S(1)}, bf16[32,768]{1,0:T(8,128)(2,1)S(1)}, u32[]{:S(2)}, u32[]{:S(2)}) collective-permute-start(bf16[32,768]{1,0:T(8,128)(2,1)S(1)} %copy-done.6), channel_id=1, source_target_pairs={{0,32},{32,0},{64,96},{96,64},{1,33},{33,1},{65,97},{97,65},{2,34}... | collective-permute-start | bytes 147464 | tf_op jit(solution)/shard_map/ppermute | solution.py:318
  29.6 7.0 %collective-permute-start.3 = (bf16[32,768]{1,0:T(8,128)(2,1)S(1)}, bf16[32,768]{1,0:T(8,128)(2,1)S(1)}, u32[]{:S(2)}, u32[]{:S(2)}) collective-permute-start(bf16[32,768]{1,0:T(8,128)(2,1)S(1)} %copy-done.6), channel_id=1, source_target_pairs={{0,96},{32,64},{64,32},{96,0},{1,97},{33,65},{65,33},{97,1},{2,98}... | collective-permute-start | bytes 147464 | tf_op jit(solution)/shard_map/ppermute | solution.py:318
  36.6 2.6 %collective-permute-start = (bf16[128,768]{1,0:T(8,128)(2,1)S(1)}, bf16[128,768]{1,0:T(8,128)(2,1)S(1)}, u32[]{:S(2)}, u32[]{:S(2)}) collective-permute-start(bf16[128,768]{1,0:T(8,128)(2,1)S(1)} %copy-done.3), channel_id=1, source_target_pairs={{0,16},{16,0},{1,17},{17,1},{2,18},{18,2},{3,19},{19,3},{4,20},{20... | collective-permute-start | bytes 589832 | tf_op jit(solution)/shard_map/ppermute | solution.py:313
  39.3 0.1 pad_add_fusion.where_ref
  39.3 0.8 collective-permute-done.3
  40.2 0.0 copy-start.5
  40.2 4.0 %collective-permute-done = bf16[128,768]{1,0:T(8,128)(2,1)S(1)} collective-permute-done((bf16[128,768]{1,0:T(8,128)(2,1)S(1)}, bf16[128,768]{1,0:T(8,128)(2,1)S(1)}, u32[]{:S(2)}, u32[]{:S(2)}) %collective-permute-start) | collective-permute-done | bytes 196640 | tf_op jit(solution)/shard_map/ppermute | solution.py:313
  44.3 0.3 split.1
  44.5 1.9 %collective-permute-start.4 = (bf16[128,768]{1,0:T(8,128)(2,1)S(1)}, bf16[128,768]{1,0:T(8,128)(2,1)S(1)}, u32[]{:S(2)}, u32[]{:S(2)}) collective-permute-start(bf16[128,768]{1,0:T(8,128)(2,1)S(1)} %get-tuple-element.17), channel_id=1, source_target_pairs={{0,16},{16,0},{1,17},{17,1},{2,18},{18,2},{3,19},{19,3},{4,20},{20... | collective-permute-start | bytes 589832 | tf_op jit(solution)/shard_map/ppermute | solution.py:313
  46.5 5.0 %all_gather.12.near_ref.near_rows_ref = bf16[512,768]{1,0:T(8,128)(2,1)S(1)} all-gather(bf16[256,768]{1,0:T(8,128)(2,1)S(1)} %pad_maximum_fusion), channel_id=1, replica_groups=mesh['yh'=2,'zh'=2,'zm'=4,'zl'=2,'c'=2,'dp'=8] {'c'}, dimensions={0}, use_global_device_ids=true | all-gather | bytes 1179648 | tf_op jit(solution)/shard_map/all_gather | solution.py:314
  51.5 2.9 %collective-permute-start.5 = (bf16[128,768]{1,0:T(8,128)(2,1)S(1)}, bf16[128,768]{1,0:T(8,128)(2,1)S(1)}, u32[]{:S(2)}, u32[]{:S(2)}) collective-permute-start(bf16[128,768]{1,0:T(8,128)(2,1)S(1)} %get-tuple-element.20), channel_id=1, source_target_pairs={{0,16},{16,0},{1,17},{17,1},{2,18},{18,2},{3,19},{19,3},{4,20},{20... | collective-permute-start | bytes 589832 | tf_op jit(solution)/shard_map/ppermute | solution.py:313
  54.5 0.0 copy-start
  54.5 0.0 copy-start.1
  54.5 2.8 %all_gather.13.back_ref = bf16[512,768]{1,0:T(8,128)(2,1)S(1)} all-gather(bf16[256,768]{1,0:T(8,128)(2,1)S(1)} %pad_maximum_fusion.1), channel_id=1, replica_groups=mesh['yh'=2,'zh'=2,'zm'=4,'zl'=2,'c'=2,'dp'=8] {'c'}, dimensions={0}, use_global_device_ids=true | all-gather | bytes 1179648 | tf_op jit(solution)/shard_map/all_gather | solution.py:314
  57.3 3.2 %stats.1 = f32[128,128]{1,0:T(8,128)} custom-call(s32[4,12]{1,0:T(4,128)S(1)} %copy-done.7, bf16[128,768]{1,0:T(8,128)(2,1)S(1)} %copy-done.1, bf16[128,768]{1,0:T(8,128)(2,1)S(1)} %copy-done.2, bf16[128,768]{1,0:T(8,128)(2,1)S(1)} %copy-done.3, bf16[32,768]{1,0:T(8,128)(2,1)S(1)} %copy-done.6, bf16[128,768]{1,0:T(8,128)(2,1)S(1)} %copy-done, ...), custom_call_target="tpu_custom_call" | custom-call | flops 200000000 | bytes 2000000 | tf_op jit(solution)/shard_map/stats/pallas_call | solution.py:348
  60.4 6.8 %all-to-all-start.1 = ((f32[16,8,128]{2,1,0:T(8,128)}), f32[16,8,128]{2,1,0:T(8,128)S(1)}, u32[]{:S(2)}, u32[]{:S(2)}) async-start(f32[16,8,128]{2,1,0:T(8,128)} %bitcast.4), calls=%async_computation.1 | async-start | bytes 131072 | tf_op jit(solution)/shard_map/all_to_all | solution.py:305
  67.3 4.9 %forward.1 = (bf16[128,768]{1,0:T(8,128)(2,1)}, bf16[128,768]{1,0:T(8,128)(2,1)}, f32[24,128]{1,0:T(8,128)S(1)}) custom-call(s32[4,12]{1,0:T(4,128)S(1)} %copy-done.7, bf16[128,768]{1,0:T(8,128)(2,1)S(1)} %copy-done.1, bf16[128,768]{1,0:T(8,128)(2,1)S(1)} %copy-done.2, bf16[128,768]{1,0:T(8,128)(2,1)S(1)} %copy-done.4, bf16[128,768]{1,0:T(8,128)(2,1)S(1)} %copy-done.5, ...), custom_call_target="tpu_custom_call" | custom-call | flops 1000000000 | bytes 3000000 | tf_op jit(solution)/shard_map/forward/pallas_call | solution.py:357
  72.2 2.8 %all_gather.14.back_ref = bf16[512,768]{1,0:T(8,128)(2,1)S(1)} all-gather(bf16[256,768]{1,0:T(8,128)(2,1)S(1)} %pad_maximum_fusion.2), channel_id=1, replica_groups=mesh['yh'=2,'zh'=2,'zm'=4,'zl'=2,'c'=2,'dp'=8] {'c'}, dimensions={0}, use_global_device_ids=true | all-gather | bytes 1179648 | tf_op jit(solution)/shard_map/all_gather | solution.py:314
  75.0 2.4 %all-to-all-done.1 = f32[16,8,128]{2,1,0:T(8,128)S(1)} async-done(((f32[16,8,128]{2,1,0:T(8,128)}), f32[16,8,128]{2,1,0:T(8,128)S(1)}, u32[]{:S(2)}, u32[]{:S(2)}) %all-to-all-start.1) | async-done | bytes 65568 | tf_op jit(solution)/shard_map/all_to_all | solution.py:305
  77.4 7.5 %all_gather.15.stat_ref = f32[512,128]{1,0:T(8,128)S(1)} all-gather(f32[128,128]{1,0:T(8,128)S(1)} %bitcast.8), channel_id=1, replica_groups=mesh['yh'=2,'zh'=2,'zm'=4,'zl'=2,'c'=2,'dp'=8] {'zl','c'}, dimensions={0}, use_global_device_ids=true | all-gather | bytes 327680 | tf_op jit(solution)/shard_map/all_gather | solution.py:309
  84.9 3.5 %backward.1 = (bf16[128,768]{1,0:T(8,128)(2,1)}, bf16[128,768]{1,0:T(8,128)(2,1)}) custom-call(s32[4,12]{1,0:T(4,128)S(1)} %copy-done.7, s32[2]{0:T(128)S(1)} %pad_add_fusion.where_ref, bf16[128,768]{1,0:T(8,128)(2,1)S(1)} %copy-done.1, bf16[128,768]{1,0:T(8,128)(2,1)S(1)} %copy-done.2, bf16[128,768]{1,0:T(8,128)(2,1)S(1)} %copy-done.4, ...), custom_call_target="tpu_custom_call" | custom-call | flops 1000000000 | bytes 3000000 | tf_op jit(solution)/shard_map/backward/pallas_call | solution.py:372
  (22 shorter events, 0.1 us)
Async XLA Ops:
  3.7 19.7 %copy-start.6 = (bf16[32,768]{1,0:T(8,128)(2,1)S(1)}, bf16[32,768]{1,0:T(8,128)(2,1)}, u32[]{:S(2)}) copy-start(bf16[32,768]{1,0:T(8,128)(2,1)} %get-tuple-element.16.mid_ref) | copy-start | bytes 147460
  3.7 32.9 %copy-start.3 = (bf16[128,768]{1,0:T(8,128)(2,1)S(1)}, bf16[128,768]{1,0:T(8,128)(2,1)}, u32[]{:S(2)}) copy-start(bf16[128,768]{1,0:T(8,128)(2,1)} %get-tuple-element.14.near_ref) | copy-start | bytes 589828
  3.7 40.5 %all-to-all-start = ((bf16[16,8,768]{2,1,0:T(8,128)(2,1)}), bf16[16,8,768]{2,1,0:T(8,128)(2,1)S(1)}, u32[]{:S(2)}, u32[]{:S(2)}) async-start(bf16[16,8,768]{2,1,0:T(8,128)(2,1)} %bitcast.6), calls=%async_computation | async-start | bytes 393216 | tf_op jit(solution)/shard_map/all_to_all | solution.py:305
  23.4 16.0 %collective-permute-start.1 = (bf16[32,768]{1,0:T(8,128)(2,1)S(1)}, bf16[32,768]{1,0:T(8,128)(2,1)S(1)}, u32[]{:S(2)}, u32[]{:S(2)}) collective-permute-start(bf16[32,768]{1,0:T(8,128)(2,1)S(1)} %copy-done.6), channel_id=1, source_target_pairs={{0,64},{32,96},{64,0},{96,32},{1,65},{33,97},{65,1},{97,33},{2,66}... | collective-permute-start | bytes 147464 | tf_op jit(solution)/shard_map/ppermute | solution.py:318
  27.4 12.0 %collective-permute-start.2 = (bf16[32,768]{1,0:T(8,128)(2,1)S(1)}, bf16[32,768]{1,0:T(8,128)(2,1)S(1)}, u32[]{:S(2)}, u32[]{:S(2)}) collective-permute-start(bf16[32,768]{1,0:T(8,128)(2,1)S(1)} %copy-done.6), channel_id=1, source_target_pairs={{0,32},{32,0},{64,96},{96,64},{1,33},{33,1},{65,97},{97,65},{2,34}... | collective-permute-start | bytes 147464 | tf_op jit(solution)/shard_map/ppermute | solution.py:318
  29.6 10.6 %collective-permute-start.3 = (bf16[32,768]{1,0:T(8,128)(2,1)S(1)}, bf16[32,768]{1,0:T(8,128)(2,1)S(1)}, u32[]{:S(2)}, u32[]{:S(2)}) collective-permute-start(bf16[32,768]{1,0:T(8,128)(2,1)S(1)} %copy-done.6), channel_id=1, source_target_pairs={{0,96},{32,64},{64,32},{96,0},{1,97},{33,65},{65,33},{97,1},{2,98}... | collective-permute-start | bytes 147464 | tf_op jit(solution)/shard_map/ppermute | solution.py:318
  36.6 7.6 %collective-permute-start = (bf16[128,768]{1,0:T(8,128)(2,1)S(1)}, bf16[128,768]{1,0:T(8,128)(2,1)S(1)}, u32[]{:S(2)}, u32[]{:S(2)}) collective-permute-start(bf16[128,768]{1,0:T(8,128)(2,1)S(1)} %copy-done.3), channel_id=1, source_target_pairs={{0,16},{16,0},{1,17},{17,1},{2,18},{18,2},{3,19},{19,3},{4,20},{20... | collective-permute-start | bytes 589832 | tf_op jit(solution)/shard_map/ppermute | solution.py:313
  40.1 4.1 %copy-start.4 = (bf16[128,768]{1,0:T(8,128)(2,1)S(1)}, bf16[128,768]{1,0:T(8,128)(2,1)}, u32[]{:S(2)}) copy-start(bf16[128,768]{1,0:T(8,128)(2,1)} %q_ref.5) | copy-start | bytes 589828
  40.2 4.1 %copy-start.5 = (bf16[128,768]{1,0:T(8,128)(2,1)S(1)}, bf16[128,768]{1,0:T(8,128)(2,1)}, u32[]{:S(2)}) copy-start(bf16[128,768]{1,0:T(8,128)(2,1)} %g_ref.5) | copy-start | bytes 589828
  44.5 9.9 %collective-permute-start.4 = (bf16[128,768]{1,0:T(8,128)(2,1)S(1)}, bf16[128,768]{1,0:T(8,128)(2,1)S(1)}, u32[]{:S(2)}, u32[]{:S(2)}) collective-permute-start(bf16[128,768]{1,0:T(8,128)(2,1)S(1)} %get-tuple-element.17), channel_id=1, source_target_pairs={{0,16},{16,0},{1,17},{17,1},{2,18},{18,2},{3,19},{19,3},{4,20},{20... | collective-permute-start | bytes 589832 | tf_op jit(solution)/shard_map/ppermute | solution.py:313
  51.5 15.7 %collective-permute-start.5 = (bf16[128,768]{1,0:T(8,128)(2,1)S(1)}, bf16[128,768]{1,0:T(8,128)(2,1)S(1)}, u32[]{:S(2)}, u32[]{:S(2)}) collective-permute-start(bf16[128,768]{1,0:T(8,128)(2,1)S(1)} %get-tuple-element.20), channel_id=1, source_target_pairs={{0,16},{16,0},{1,17},{17,1},{2,18},{18,2},{3,19},{19,3},{4,20},{20... | collective-permute-start | bytes 589832 | tf_op jit(solution)/shard_map/ppermute | solution.py:313
  54.5 2.8 %copy-start = (bf16[128,768]{1,0:T(8,128)(2,1)S(1)}, bf16[128,768]{1,0:T(8,128)(2,1)}, u32[]{:S(2)}) copy-start(bf16[128,768]{1,0:T(8,128)(2,1)} %get-tuple-element.15.far_ref) | copy-start | bytes 589828
  54.5 2.8 %copy-start.1 = (bf16[128,768]{1,0:T(8,128)(2,1)S(1)}, bf16[128,768]{1,0:T(8,128)(2,1)}, u32[]{:S(2)}) copy-start(bf16[128,768]{1,0:T(8,128)(2,1)} %k_ref.5) | copy-start | bytes 589828
  54.5 2.8 %copy-start.2 = (bf16[128,768]{1,0:T(8,128)(2,1)S(1)}, bf16[128,768]{1,0:T(8,128)(2,1)}, u32[]{:S(2)}) copy-start(bf16[128,768]{1,0:T(8,128)(2,1)} %v_ref.5) | copy-start | bytes 589828
  54.5 2.8 %copy-start.7 = (s32[4,12]{1,0:T(4,128)S(1)}, s32[4,12]{1,0:T(4,128)}, u32[]{:S(2)}) copy-start(s32[4,12]{1,0:T(4,128)} %off_ref.7) | copy-start | bytes 580
  60.4 16.9 %all-to-all-start.1 = ((f32[16,8,128]{2,1,0:T(8,128)}), f32[16,8,128]{2,1,0:T(8,128)S(1)}, u32[]{:S(2)}, u32[]{:S(2)}) async-start(f32[16,8,128]{2,1,0:T(8,128)} %bitcast.4), calls=%async_computation.1 | async-start | bytes 131072 | tf_op jit(solution)/shard_map/all_to_all | solution.py:305

commit v4 on v3

--- a/solution.py
+++ b/solution.py
@@ -21,8 +21,10 @@
 N_NEAR = 4
 ROWS1, ROWS2, ROWS3 = 32, 8, 2
 NEG = -1e30
+STAGED = 6
+STAGED_FORWARD = 3
 CUTS = 4
-ROOT_ROWS, ROOT_STATS = 13, 2
+ROOT_ROWS, ROOT_STATS = 13, 3
 F32 = jnp.float32
 BF16 = jnp.bfloat16
 VMEM = pl.BlockSpec(memory_space=pltpu.VMEM)
@@ -157,7 +159,7 @@
     def pick(level, pair):
         return jnp.where(both < 48, off_ref[level, 2 * pair], off_ref[level, 2 * pair + 1])
 
-    for pair in range(PAIRS):
+    def scores_of(pair):
         cols = lanes(pair)
         far = far_ref[:16, cols].astype(F32)[:8]
         mid = mid_ref[16:, cols].astype(F32)
@@ -165,33 +167,50 @@
         query = jnp.concatenate([near[:32], mid[:8], pltpu.roll(far, 4, 0)], 0).astype(BF16)
         grad = stacked(jnp.concatenate([near[32:], mid[8:], pltpu.roll(far, 2, 0)], 0))
         keys = gathered(k_ref, near_rows_ref, back_ref, 0, pair)
-        values = gathered(v_ref, near_rows_ref, back_ref, 1, pair)
+        return dot_t(stacked(query), keys) * SCALE, grad
+
+    def weights_of(pair, scores):
         tok = jnp.where(
             slot < 32,
             slot * 4 + pick(1, pair),
             jnp.where(slot < 40, (slot - 32) * 16 + pick(2, pair), slot % 2 * 64 + pick(3, pair)),
         )
         live = [chosen(off_ref, pair, level, tok) for level in range(1, 4)]
-        raw, total, top = softmax(dot_t(stacked(query), keys) * SCALE, live)
-        out = (dot(raw.astype(BF16), values) * (1.0 / total)).astype(BF16).astype(F32)
-        delta = jnp.sum(grad * out, axis=1, keepdims=True)
-        logs = top + jnp.log(total)
-        turn = pair // 2
-        lane = jnp.where(
-            row < 32,
-            row + 32 * turn,
-            jnp.where(
-                row < 40, row + 64 + 8 * turn, jnp.where(row < 42, row + 80 + 2 * turn, -1)
-            ),
-        )
-        hit = iota((48, 128), 1) == lane
-        for side in range(2):
-            for kind, column in enumerate((logs, delta)):
-                line = jnp.sum(
-                    jnp.where(hit, column[side * 48 : side * 48 + 48], 0.0), axis=0, keepdims=True
-                )
-                place = 2 * ((2 * pair + side) % 4) + kind
-                sums[place] = line if sums[place] is None else sums[place] + line
+        raw, total, top = softmax(scores, live)
+        return raw.astype(BF16), total, top
+
+    def columns_of(pair, grad, raw, total, top):
+        values = gathered(v_ref, near_rows_ref, back_ref, 1, pair)
+        out = (dot(raw, values) * (1.0 / total)).astype(BF16).astype(F32)
+        return top + jnp.log(total), jnp.sum(grad * out, axis=1, keepdims=True)
+
+    for first in range(0, PAIRS, STAGED):
+        pairs = range(first, first + STAGED)
+        scores = [scores_of(pair) for pair in pairs]
+        weights = [weights_of(pair, part[0]) for pair, part in zip(pairs, scores)]
+        columns = [
+            columns_of(pair, part[1], *weight)
+            for pair, part, weight in zip(pairs, scores, weights)
+        ]
+        for pair, (logs, delta) in zip(pairs, columns):
+            turn = pair // 2
+            lane = jnp.where(
+                row < 32,
+                row + 32 * turn,
+                jnp.where(
+                    row < 40, row + 64 + 8 * turn, jnp.where(row < 42, row + 80 + 2 * turn, -1)
+                ),
+            )
+            hit = iota((48, 128), 1) == lane
+            for side in range(2):
+                for kind, column in enumerate((logs, delta)):
+                    line = jnp.sum(
+                        jnp.where(hit, column[side * 48 : side * 48 + 48], 0.0),
+                        axis=0,
+                        keepdims=True,
+                    )
+                    place = 2 * ((2 * pair + side) % 4) + kind
+                    sums[place] = line if sums[place] is None else sums[place] + line
     stat_ref[...] = jnp.concatenate(sums * N_FAR, 0)
 
 
@@ -200,30 +219,44 @@
 ):
     eye = iota((TOK, 128), 0) == iota((TOK, 128), 1)
     row = iota((2 * TOK, 128), 0)
-    for pair in range(PAIRS):
+    def products(pair):
         keys = gathered(k_ref, near_ref, back_ref, 0, pair)
         values = gathered(v_ref, near_ref, back_ref, 1, pair)
         grad = stacked(g_ref[:, lanes(pair)])
         scores = dot_t(stacked(q_ref[:, lanes(pair)]), keys) * SCALE
-        live = [chosen(off_ref, pair, level, row) for level in range(1, 4)]
-        raw, total, top = softmax(scores, live)
+        return keys, values, grad, scores
+
+    def weights(pair, scores):
+        return softmax(scores, [chosen(off_ref, pair, level, row) for level in range(1, 4)])
+
+    def outputs(pair, values, grad, raw, total):
         inverse = 1.0 / total
         out = halves(dot(raw.astype(BF16), values) * inverse).astype(BF16)
         att_ref[:, lanes(pair)] = out
         out = out.astype(F32)
         delta = jnp.sum(grad.astype(F32) * jnp.concatenate([out, out], 0), axis=1, keepdims=True)
         grad_probs = dot_t(grad, values)
-        grad_scores = (raw * inverse * (grad_probs - delta)).astype(BF16)
-        gq_ref[:, lanes(pair)] = halves(dot(grad_scores, keys) * SCALE).astype(BF16)
-        logs = top + jnp.log(total)
-        for side in range(2):
-            head = 2 * pair + side
-            for kind, column in enumerate((logs, delta)):
-                own_ref[2 * head + kind : 2 * head + kind + 1, :] = jnp.sum(
-                    jnp.where(eye, column[side * TOK : side * TOK + TOK], 0.0),
-                    axis=0,
-                    keepdims=True,
-                )
+        return delta, (raw * inverse * (grad_probs - delta)).astype(BF16)
+
+    for first in range(0, PAIRS, STAGED_FORWARD):
+        pairs = range(first, first + STAGED_FORWARD)
+        parts = [products(pair) for pair in pairs]
+        soft = [weights(pair, part[3]) for pair, part in zip(pairs, parts)]
+        done = [
+            outputs(pair, part[1], part[2], raw, total)
+            for pair, part, (raw, total, _) in zip(pairs, parts, soft)
+        ]
+        for pair, part, (_, total, top), (delta, grad_scores) in zip(pairs, parts, soft, done):
+            gq_ref[:, lanes(pair)] = halves(dot(grad_scores, part[0]) * SCALE).astype(BF16)
+            logs = top + jnp.log(total)
+            for side in range(2):
+                head = 2 * pair + side
+                for kind, column in enumerate((logs, delta)):
+                    own_ref[2 * head + kind : 2 * head + kind + 1, :] = jnp.sum(
+                        jnp.where(eye, column[side * TOK : side * TOK + TOK], 0.0),
+                        axis=0,
+                        keepdims=True,
+                    )
 
 
 def backward_kernel(

time: 88.9 us -> 87.1 us (0.980)
  Pallas kernels: 14.8 us -> 12.7 us
  starting transfers between devices: 47.1 us -> 48.7 us
  waiting for transfers between devices: 7.25 us -> 6.34 us
    all_to_all x2, starting transfers between devices: 26.5 us -> 28.1 us  [to_far(): return lax.all_to_all(value, FAR, 0, 0, tiled=True, axis_index_groups=order)]
    pallas_call x1, Pallas kernels: 4.86 us -> 3.76 us  [on_device(): pl.pallas_call(forward_kernel, name='forward', out_shape=(shape(TOK, FULL...]
    pallas_call x1, Pallas kernels: 3.15 us -> 2.11 us  [on_device(): pl.pallas_call(stat_kernel, name='stats', out_shape=shape(8 * N_FAR, 128,...]
    all_to_all x2, waiting for transfers between devices: 2.42 us -> 1.51 us  [to_far(): return lax.all_to_all(value, FAR, 0, 0, tiled=True, axis_index_groups=order)]
  transfers between devices with their start and end apart: 8 -> 8, of which waited for: 3 -> 3; matrix products, arithmetic and copies ran while one was open for 0% -> 0% of each run, Pallas kernels for 9% -> 7%
where the time goes in v4:
time: 87.1 us; the launch traced here: 86.6 us
  starting transfers between devices  48.7 us (56%)
  blocking collectives  17.7 us (20%)
  Pallas kernels  12.7 us (15%)
  waiting for transfers between devices  6.34 us (7%)
    all_to_all x2, starting transfers between devices, to_far(): return lax.all_to_all(value, FAR, 0, 0, tiled=True, axis_index_groups=order)  28.1 us
    ppermute x3, starting transfers between devices, swap_mid(): return lax.ppermute(value, 'zm', [(i, i ^ step) for i in range(4)])  13.2 us
    all_gather x3, blocking collectives, to_pair(): lax.all_gather(jnp.concatenate([value, other], 0), 'c', axis=0, tiled=True)  10.7 us
    ppermute x3, starting transfers between devices, to_pair(): other = lax.ppermute(value, 'zl', [(0, 1), (1, 0)])  7.46 us
    all_gather x1, blocking collectives, to_near(): return lax.all_gather(value, NEAR, axis=0, tiled=True)  6.97 us
    ppermute x3, waiting for transfers between devices, to_pair(): other = lax.ppermute(value, 'zl', [(0, 1), (1, 0)])  4.03 us
    pallas_call x1, Pallas kernels, on_device(): pl.pallas_call(forward_kernel, name='forward', out_shape=(shape(TOK, FULL...  3.76 us
    pallas_call x1, Pallas kernels, on_device(): pl.pallas_call(backward_kernel, name='backward', out_shape=(shape(TOK, FU...  3.47 us
  transfers between devices with their start and end apart: 8, of which 3 were waited for; matrix products, arithmetic and copies ran while one was open for 0% of the time, Pallas kernels for 7%

profile of v4, /device:TPU:1, one launch (start us, length us, event | category | flops | bytes accessed | tf_op | source)
XLA Modules:
  0.0 86.6 jit_solution(13773534144904328388)
XLA Ops:
  0.6 3.1 %pick.1 = (bf16[128,768]{1,0:T(8,128)(2,1)}, bf16[32,768]{1,0:T(8,128)(2,1)}, bf16[128,768]{1,0:T(8,128)(2,1)}) custom-call(s32[4,12]{1,0:T(4,128)} %off_ref.7, bf16[128,768]{1,0:T(8,128)(2,1)} %k_ref.5, bf16[128,768]{1,0:T(8,128)(2,1)} %v_ref.5, bf16[128,768]{1,0:T(8,128)(2,1)} %q_ref.5, bf16[128,768]{1,0:T(8,128)(2,1)} %g_ref.5), custom_call_target="tpu_custom_call" | custom-call | flops 200000000 | bytes 1100000 | tf_op jit(solution)/shard_map/pick/pallas_call | solution.py:358
  3.7 0.0 copy-start.6
  3.7 19.6 %all-to-all-start = ((bf16[16,8,768]{2,1,0:T(8,128)(2,1)}), bf16[16,8,768]{2,1,0:T(8,128)(2,1)S(1)}, u32[]{:S(2)}, u32[]{:S(2)}) async-start(bf16[16,8,768]{2,1,0:T(8,128)(2,1)} %bitcast.6), calls=%async_computation | async-start | bytes 393216 | tf_op jit(solution)/shard_map/all_to_all | solution.py:338
  23.4 4.0 %collective-permute-start.1 = (bf16[32,768]{1,0:T(8,128)(2,1)S(1)}, bf16[32,768]{1,0:T(8,128)(2,1)S(1)}, u32[]{:S(2)}, u32[]{:S(2)}) collective-permute-start(bf16[32,768]{1,0:T(8,128)(2,1)S(1)} %copy-done.6), channel_id=1, source_target_pairs={{0,64},{32,96},{64,0},{96,32},{1,65},{33,97},{65,1},{97,33},{2,66}... | collective-permute-start | bytes 147464 | tf_op jit(solution)/shard_map/ppermute | solution.py:351
  27.4 2.2 %collective-permute-start.2 = (bf16[32,768]{1,0:T(8,128)(2,1)S(1)}, bf16[32,768]{1,0:T(8,128)(2,1)S(1)}, u32[]{:S(2)}, u32[]{:S(2)}) collective-permute-start(bf16[32,768]{1,0:T(8,128)(2,1)S(1)} %copy-done.6), channel_id=1, source_target_pairs={{0,32},{32,0},{64,96},{96,64},{1,33},{33,1},{65,97},{97,65},{2,34}... | collective-permute-start | bytes 147464 | tf_op jit(solution)/shard_map/ppermute | solution.py:351
  29.6 7.0 %collective-permute-start.3 = (bf16[32,768]{1,0:T(8,128)(2,1)S(1)}, bf16[32,768]{1,0:T(8,128)(2,1)S(1)}, u32[]{:S(2)}, u32[]{:S(2)}) collective-permute-start(bf16[32,768]{1,0:T(8,128)(2,1)S(1)} %copy-done.6), channel_id=1, source_target_pairs={{0,96},{32,64},{64,32},{96,0},{1,97},{33,65},{65,33},{97,1},{2,98}... | collective-permute-start | bytes 147464 | tf_op jit(solution)/shard_map/ppermute | solution.py:351
  36.6 2.6 %collective-permute-start = (bf16[128,768]{1,0:T(8,128)(2,1)S(1)}, bf16[128,768]{1,0:T(8,128)(2,1)S(1)}, u32[]{:S(2)}, u32[]{:S(2)}) collective-permute-start(bf16[128,768]{1,0:T(8,128)(2,1)S(1)} %copy-done.3), channel_id=1, source_target_pairs={{0,16},{16,0},{1,17},{17,1},{2,18},{18,2},{3,19},{19,3},{4,20},{20... | collective-permute-start | bytes 589832 | tf_op jit(solution)/shard_map/ppermute | solution.py:346
  39.3 0.1 pad_add_fusion.where_ref
  39.3 0.8 collective-permute-done.3
  40.2 4.0 %collective-permute-done = bf16[128,768]{1,0:T(8,128)(2,1)S(1)} collective-permute-done((bf16[128,768]{1,0:T(8,128)(2,1)S(1)}, bf16[128,768]{1,0:T(8,128)(2,1)S(1)}, u32[]{:S(2)}, u32[]{:S(2)}) %collective-permute-start) | collective-permute-done | bytes 196640 | tf_op jit(solution)/shard_map/ppermute | solution.py:346
  44.3 0.3 split.1
  44.5 1.9 %collective-permute-start.4 = (bf16[128,768]{1,0:T(8,128)(2,1)S(1)}, bf16[128,768]{1,0:T(8,128)(2,1)S(1)}, u32[]{:S(2)}, u32[]{:S(2)}) collective-permute-start(bf16[128,768]{1,0:T(8,128)(2,1)S(1)} %get-tuple-element.17), channel_id=1, source_target_pairs={{0,16},{16,0},{1,17},{17,1},{2,18},{18,2},{3,19},{19,3},{4,20},{20... | collective-permute-start | bytes 589832 | tf_op jit(solution)/shard_map/ppermute | solution.py:346
  46.5 5.0 %all_gather.12.near_ref.near_rows_ref = bf16[512,768]{1,0:T(8,128)(2,1)S(1)} all-gather(bf16[256,768]{1,0:T(8,128)(2,1)S(1)} %pad_maximum_fusion), channel_id=1, replica_groups=mesh['yh'=2,'zh'=2,'zm'=4,'zl'=2,'c'=2,'dp'=8] {'c'}, dimensions={0}, use_global_device_ids=true | all-gather | bytes 1179648 | tf_op jit(solution)/shard_map/all_gather | solution.py:347
  51.5 2.9 %collective-permute-start.5 = (bf16[128,768]{1,0:T(8,128)(2,1)S(1)}, bf16[128,768]{1,0:T(8,128)(2,1)S(1)}, u32[]{:S(2)}, u32[]{:S(2)}) collective-permute-start(bf16[128,768]{1,0:T(8,128)(2,1)S(1)} %get-tuple-element.20), channel_id=1, source_target_pairs={{0,16},{16,0},{1,17},{17,1},{2,18},{18,2},{3,19},{19,3},{4,20},{20... | collective-permute-start | bytes 589832 | tf_op jit(solution)/shard_map/ppermute | solution.py:346
  54.5 0.0 copy-start
  54.5 0.0 copy-start.1
  54.5 2.8 %all_gather.13.back_ref = bf16[512,768]{1,0:T(8,128)(2,1)S(1)} all-gather(bf16[256,768]{1,0:T(8,128)(2,1)S(1)} %pad_maximum_fusion.1), channel_id=1, replica_groups=mesh['yh'=2,'zh'=2,'zm'=4,'zl'=2,'c'=2,'dp'=8] {'c'}, dimensions={0}, use_global_device_ids=true | all-gather | bytes 1179648 | tf_op jit(solution)/shard_map/all_gather | solution.py:347
  57.3 2.1 %stats.1 = f32[128,128]{1,0:T(8,128)} custom-call(s32[4,12]{1,0:T(4,128)S(1)} %copy-done.7, bf16[128,768]{1,0:T(8,128)(2,1)S(1)} %copy-done.1, bf16[128,768]{1,0:T(8,128)(2,1)S(1)} %copy-done.2, bf16[128,768]{1,0:T(8,128)(2,1)S(1)} %copy-done.3, bf16[32,768]{1,0:T(8,128)(2,1)S(1)} %copy-done.6, bf16[128,768]{1,0:T(8,128)(2,1)S(1)} %copy-done, ...), custom_call_target="tpu_custom_call" | custom-call | flops 200000000 | bytes 2000000 | tf_op jit(solution)/shard_map/stats/pallas_call | solution.py:381
  59.4 8.5 %all-to-all-start.1 = ((f32[16,8,128]{2,1,0:T(8,128)}), f32[16,8,128]{2,1,0:T(8,128)S(1)}, u32[]{:S(2)}, u32[]{:S(2)}) async-start(f32[16,8,128]{2,1,0:T(8,128)} %bitcast.4), calls=%async_computation.1 | async-start | bytes 131072 | tf_op jit(solution)/shard_map/all_to_all | solution.py:338
  67.9 3.8 %forward.1 = (bf16[128,768]{1,0:T(8,128)(2,1)}, bf16[128,768]{1,0:T(8,128)(2,1)}, f32[24,128]{1,0:T(8,128)S(1)}) custom-call(s32[4,12]{1,0:T(4,128)S(1)} %copy-done.7, bf16[128,768]{1,0:T(8,128)(2,1)S(1)} %copy-done.1, bf16[128,768]{1,0:T(8,128)(2,1)S(1)} %copy-done.2, bf16[128,768]{1,0:T(8,128)(2,1)S(1)} %copy-done.4, bf16[128,768]{1,0:T(8,128)(2,1)S(1)} %copy-done.5, ...), custom_call_target="tpu_custom_call" | custom-call | flops 1000000000 | bytes 3000000 | tf_op jit(solution)/shard_map/forward/pallas_call | solution.py:390
  71.7 2.9 %all_gather.14.back_ref = bf16[512,768]{1,0:T(8,128)(2,1)S(1)} all-gather(bf16[256,768]{1,0:T(8,128)(2,1)S(1)} %pad_maximum_fusion.2), channel_id=1, replica_groups=mesh['yh'=2,'zh'=2,'zm'=4,'zl'=2,'c'=2,'dp'=8] {'c'}, dimensions={0}, use_global_device_ids=true | all-gather | bytes 1179648 | tf_op jit(solution)/shard_map/all_gather | solution.py:347
  74.6 1.5 %all-to-all-done.1 = f32[16,8,128]{2,1,0:T(8,128)S(1)} async-done(((f32[16,8,128]{2,1,0:T(8,128)}), f32[16,8,128]{2,1,0:T(8,128)S(1)}, u32[]{:S(2)}, u32[]{:S(2)}) %all-to-all-start.1) | async-done | bytes 65568 | tf_op jit(solution)/shard_map/all_to_all | solution.py:338
  76.1 7.0 %all_gather.15.stat_ref = f32[512,128]{1,0:T(8,128)S(1)} all-gather(f32[128,128]{1,0:T(8,128)S(1)} %bitcast.8), channel_id=1, replica_groups=mesh['yh'=2,'zh'=2,'zm'=4,'zl'=2,'c'=2,'dp'=8] {'zl','c'}, dimensions={0}, use_global_device_ids=true | all-gather | bytes 327680 | tf_op jit(solution)/shard_map/all_gather | solution.py:342
  83.1 3.5 %backward.1 = (bf16[128,768]{1,0:T(8,128)(2,1)}, bf16[128,768]{1,0:T(8,128)(2,1)}) custom-call(s32[4,12]{1,0:T(4,128)S(1)} %copy-done.7, s32[2]{0:T(128)S(1)} %pad_add_fusion.where_ref, bf16[128,768]{1,0:T(8,128)(2,1)S(1)} %copy-done.1, bf16[128,768]{1,0:T(8,128)(2,1)S(1)} %copy-done.2, bf16[128,768]{1,0:T(8,128)(2,1)S(1)} %copy-done.4, ...), custom_call_target="tpu_custom_call" | custom-call | flops 1000000000 | bytes 3000000 | tf_op jit(solution)/shard_map/backward/pallas_call | solution.py:405
  (22 shorter events, 0.1 us)
Async XLA Ops:
  3.7 19.7 %copy-start.6 = (bf16[32,768]{1,0:T(8,128)(2,1)S(1)}, bf16[32,768]{1,0:T(8,128)(2,1)}, u32[]{:S(2)}) copy-start(bf16[32,768]{1,0:T(8,128)(2,1)} %get-tuple-element.16.mid_ref) | copy-start | bytes 147460
  3.7 32.9 %copy-start.3 = (bf16[128,768]{1,0:T(8,128)(2,1)S(1)}, bf16[128,768]{1,0:T(8,128)(2,1)}, u32[]{:S(2)}) copy-start(bf16[128,768]{1,0:T(8,128)(2,1)} %get-tuple-element.14.near_ref) | copy-start | bytes 589828
  3.7 40.5 %all-to-all-start = ((bf16[16,8,768]{2,1,0:T(8,128)(2,1)}), bf16[16,8,768]{2,1,0:T(8,128)(2,1)S(1)}, u32[]{:S(2)}, u32[]{:S(2)}) async-start(bf16[16,8,768]{2,1,0:T(8,128)(2,1)} %bitcast.6), calls=%async_computation | async-start | bytes 393216 | tf_op jit(solution)/shard_map/all_to_all | solution.py:338
  23.4 16.0 %collective-permute-start.1 = (bf16[32,768]{1,0:T(8,128)(2,1)S(1)}, bf16[32,768]{1,0:T(8,128)(2,1)S(1)}, u32[]{:S(2)}, u32[]{:S(2)}) collective-permute-start(bf16[32,768]{1,0:T(8,128)(2,1)S(1)} %copy-done.6), channel_id=1, source_target_pairs={{0,64},{32,96},{64,0},{96,32},{1,65},{33,97},{65,1},{97,33},{2,66}... | collective-permute-start | bytes 147464 | tf_op jit(solution)/shard_map/ppermute | solution.py:351
  27.4 12.0 %collective-permute-start.2 = (bf16[32,768]{1,0:T(8,128)(2,1)S(1)}, bf16[32,768]{1,0:T(8,128)(2,1)S(1)}, u32[]{:S(2)}, u32[]{:S(2)}) collective-permute-start(bf16[32,768]{1,0:T(8,128)(2,1)S(1)} %copy-done.6), channel_id=1, source_target_pairs={{0,32},{32,0},{64,96},{96,64},{1,33},{33,1},{65,97},{97,65},{2,34}... | collective-permute-start | bytes 147464 | tf_op jit(solution)/shard_map/ppermute | solution.py:351
  29.6 10.6 %collective-permute-start.3 = (bf16[32,768]{1,0:T(8,128)(2,1)S(1)}, bf16[32,768]{1,0:T(8,128)(2,1)S(1)}, u32[]{:S(2)}, u32[]{:S(2)}) collective-permute-start(bf16[32,768]{1,0:T(8,128)(2,1)S(1)} %copy-done.6), channel_id=1, source_target_pairs={{0,96},{32,64},{64,32},{96,0},{1,97},{33,65},{65,33},{97,1},{2,98}... | collective-permute-start | bytes 147464 | tf_op jit(solution)/shard_map/ppermute | solution.py:351
  36.6 7.6 %collective-permute-start = (bf16[128,768]{1,0:T(8,128)(2,1)S(1)}, bf16[128,768]{1,0:T(8,128)(2,1)S(1)}, u32[]{:S(2)}, u32[]{:S(2)}) collective-permute-start(bf16[128,768]{1,0:T(8,128)(2,1)S(1)} %copy-done.3), channel_id=1, source_target_pairs={{0,16},{16,0},{1,17},{17,1},{2,18},{18,2},{3,19},{19,3},{4,20},{20... | collective-permute-start | bytes 589832 | tf_op jit(solution)/shard_map/ppermute | solution.py:346
  40.1 4.1 %copy-start.4 = (bf16[128,768]{1,0:T(8,128)(2,1)S(1)}, bf16[128,768]{1,0:T(8,128)(2,1)}, u32[]{:S(2)}) copy-start(bf16[128,768]{1,0:T(8,128)(2,1)} %q_ref.5) | copy-start | bytes 589828
  40.2 4.1 %copy-start.5 = (bf16[128,768]{1,0:T(8,128)(2,1)S(1)}, bf16[128,768]{1,0:T(8,128)(2,1)}, u32[]{:S(2)}) copy-start(bf16[128,768]{1,0:T(8,128)(2,1)} %g_ref.5) | copy-start | bytes 589828
  44.5 9.9 %collective-permute-start.4 = (bf16[128,768]{1,0:T(8,128)(2,1)S(1)}, bf16[128,768]{1,0:T(8,128)(2,1)S(1)}, u32[]{:S(2)}, u32[]{:S(2)}) collective-permute-start(bf16[128,768]{1,0:T(8,128)(2,1)S(1)} %get-tuple-element.17), channel_id=1, source_target_pairs={{0,16},{16,0},{1,17},{17,1},{2,18},{18,2},{3,19},{19,3},{4,20},{20... | collective-permute-start | bytes 589832 | tf_op jit(solution)/shard_map/ppermute | solution.py:346
  51.5 16.4 %collective-permute-start.5 = (bf16[128,768]{1,0:T(8,128)(2,1)S(1)}, bf16[128,768]{1,0:T(8,128)(2,1)S(1)}, u32[]{:S(2)}, u32[]{:S(2)}) collective-permute-start(bf16[128,768]{1,0:T(8,128)(2,1)S(1)} %get-tuple-element.20), channel_id=1, source_target_pairs={{0,16},{16,0},{1,17},{17,1},{2,18},{18,2},{3,19},{19,3},{4,20},{20... | collective-permute-start | bytes 589832 | tf_op jit(solution)/shard_map/ppermute | solution.py:346
  54.5 2.8 %copy-start = (bf16[128,768]{1,0:T(8,128)(2,1)S(1)}, bf16[128,768]{1,0:T(8,128)(2,1)}, u32[]{:S(2)}) copy-start(bf16[128,768]{1,0:T(8,128)(2,1)} %get-tuple-element.15.far_ref) | copy-start | bytes 589828
  54.5 2.8 %copy-start.1 = (bf16[128,768]{1,0:T(8,128)(2,1)S(1)}, bf16[128,768]{1,0:T(8,128)(2,1)}, u32[]{:S(2)}) copy-start(bf16[128,768]{1,0:T(8,128)(2,1)} %k_ref.5) | copy-start | bytes 589828
  54.5 2.8 %copy-start.2 = (bf16[128,768]{1,0:T(8,128)(2,1)S(1)}, bf16[128,768]{1,0:T(8,128)(2,1)}, u32[]{:S(2)}) copy-start(bf16[128,768]{1,0:T(8,128)(2,1)} %v_ref.5) | copy-start | bytes 589828
  54.5 2.8 %copy-start.7 = (s32[4,12]{1,0:T(4,128)S(1)}, s32[4,12]{1,0:T(4,128)}, u32[]{:S(2)}) copy-start(s32[4,12]{1,0:T(4,128)} %off_ref.7) | copy-start | bytes 580
  59.4 16.7 %all-to-all-start.1 = ((f32[16,8,128]{2,1,0:T(8,128)}), f32[16,8,128]{2,1,0:T(8,128)S(1)}, u32[]{:S(2)}, u32[]{:S(2)}) async-start(f32[16,8,128]{2,1,0:T(8,128)} %bitcast.4), calls=%async_computation.1 | async-start | bytes 131072 | tf_op jit(solution)/shard_map/all_to_all | solution.py:338

commit v5 on v4

--- a/solution.py
+++ b/solution.py
@@ -23,8 +23,8 @@
 NEG = -1e30
 STAGED = 6
 STAGED_FORWARD = 3
-CUTS = 4
-ROOT_ROWS, ROOT_STATS = 13, 3
+CUTS = 1
+ROOT_ROWS, ROOT_STATS = 13, 4
 F32 = jnp.float32
 BF16 = jnp.bfloat16
 VMEM = pl.BlockSpec(memory_space=pltpu.VMEM)

time: 87.1 us -> 87.5 us (level)
  starting transfers between devices: 48.7 us -> 51.8 us
  waiting for transfers between devices: 6.34 us -> 4.84 us
  blocking collectives: 17.7 us -> 16.7 us
    all_to_all x2, starting transfers between devices: 28.1 us -> 31.1 us  [to_far(): return lax.all_to_all(value, FAR, 0, 0, tiled=True, axis_index_groups=order)]
    all_to_all x2, waiting for transfers between devices: 1.51 us -> 0.01 us  [to_far(): return lax.all_to_all(value, FAR, 0, 0, tiled=True, axis_index_groups=order)]
    all_gather x1, blocking collectives: 6.97 us -> 5.98 us  [to_near(): return lax.all_gather(value, NEAR, axis=0, tiled=True)]
  transfers between devices with their start and end apart: 8 -> 8, of which waited for: 3 -> 2; matrix products, arithmetic and copies ran while one was open for 0% -> 0% of each run, Pallas kernels for 7% -> 7%
where the time goes in v5:
time: 87.5 us; the launch traced here: 87 us
  starting transfers between devices  51.8 us (59%)
  blocking collectives  16.7 us (19%)
  Pallas kernels  12.6 us (14%)
  waiting for transfers between devices  4.84 us (6%)
    all_to_all x2, starting transfers between devices, to_far(): return lax.all_to_all(value, FAR, 0, 0, tiled=True, axis_index_groups=order)  31.1 us
    ppermute x3, starting transfers between devices, swap_mid(): return lax.ppermute(value, 'zm', [(i, i ^ step) for i in range(4)])  13.2 us
    all_gather x3, blocking collectives, to_pair(): lax.all_gather(jnp.concatenate([value, other], 0), 'c', axis=0, tiled=True)  10.7 us
    ppermute x3, starting transfers between devices, to_pair(): other = lax.ppermute(value, 'zl', [(0, 1), (1, 0)])  7.45 us
    all_gather x1, blocking collectives, to_near(): return lax.all_gather(value, NEAR, axis=0, tiled=True)  5.98 us
    ppermute x3, waiting for transfers between devices, to_pair(): other = lax.ppermute(value, 'zl', [(0, 1), (1, 0)])  4.03 us
    pallas_call x1, Pallas kernels, on_device(): pl.pallas_call(forward_kernel, name='forward', out_shape=(shape(TOK, FULL...  3.76 us
    pallas_call x1, Pallas kernels, on_device(): pl.pallas_call(backward_kernel, name='backward', out_shape=(shape(TOK, FU...  3.47 us
  transfers between devices with their start and end apart: 8, of which 2 were waited for; matrix products, arithmetic and copies ran while one was open for 0% of the time, Pallas kernels for 7%

profile of v5, /device:TPU:1, one launch (start us, length us, event | category | flops | bytes accessed | tf_op | source)
XLA Modules:
  0.0 87.0 jit_solution(10342388234211288768)
XLA Ops:
  0.6 3.0 %pick.1 = (bf16[128,768]{1,0:T(8,128)(2,1)}, bf16[32,768]{1,0:T(8,128)(2,1)}, bf16[128,768]{1,0:T(8,128)(2,1)}) custom-call(s32[4,12]{1,0:T(4,128)} %off_ref.7, bf16[128,768]{1,0:T(8,128)(2,1)} %k_ref.5, bf16[128,768]{1,0:T(8,128)(2,1)} %v_ref.5, bf16[128,768]{1,0:T(8,128)(2,1)} %q_ref.5, bf16[128,768]{1,0:T(8,128)(2,1)} %g_ref.5), custom_call_target="tpu_custom_call" | custom-call | flops 200000000 | bytes 1100000 | tf_op jit(solution)/shard_map/pick/pallas_call | solution.py:358
  3.6 0.0 copy-start.6
  3.7 0.0 copy-start.3
  3.7 19.7 %all-to-all-start = ((bf16[16,8,768]{2,1,0:T(8,128)(2,1)}), bf16[16,8,768]{2,1,0:T(8,128)(2,1)S(1)}, u32[]{:S(2)}, u32[]{:S(2)}) async-start(bf16[16,8,768]{2,1,0:T(8,128)(2,1)} %bitcast.6), calls=%async_computation | async-start | bytes 393216 | tf_op jit(solution)/shard_map/all_to_all | solution.py:338
  23.3 4.0 %collective-permute-start.1 = (bf16[32,768]{1,0:T(8,128)(2,1)S(1)}, bf16[32,768]{1,0:T(8,128)(2,1)S(1)}, u32[]{:S(2)}, u32[]{:S(2)}) collective-permute-start(bf16[32,768]{1,0:T(8,128)(2,1)S(1)} %copy-done.6), channel_id=1, source_target_pairs={{0,64},{32,96},{64,0},{96,32},{1,65},{33,97},{65,1},{97,33},{2,66}... | collective-permute-start | bytes 147464 | tf_op jit(solution)/shard_map/ppermute | solution.py:351
  27.3 2.2 %collective-permute-start.2 = (bf16[32,768]{1,0:T(8,128)(2,1)S(1)}, bf16[32,768]{1,0:T(8,128)(2,1)S(1)}, u32[]{:S(2)}, u32[]{:S(2)}) collective-permute-start(bf16[32,768]{1,0:T(8,128)(2,1)S(1)} %copy-done.6), channel_id=1, source_target_pairs={{0,32},{32,0},{64,96},{96,64},{1,33},{33,1},{65,97},{97,65},{2,34}... | collective-permute-start | bytes 147464 | tf_op jit(solution)/shard_map/ppermute | solution.py:351
  29.5 7.0 %collective-permute-start.3 = (bf16[32,768]{1,0:T(8,128)(2,1)S(1)}, bf16[32,768]{1,0:T(8,128)(2,1)S(1)}, u32[]{:S(2)}, u32[]{:S(2)}) collective-permute-start(bf16[32,768]{1,0:T(8,128)(2,1)S(1)} %copy-done.6), channel_id=1, source_target_pairs={{0,96},{32,64},{64,32},{96,0},{1,97},{33,65},{65,33},{97,1},{2,98}... | collective-permute-start | bytes 147464 | tf_op jit(solution)/shard_map/ppermute | solution.py:351
  36.5 2.6 %collective-permute-start = (bf16[128,768]{1,0:T(8,128)(2,1)S(1)}, bf16[128,768]{1,0:T(8,128)(2,1)S(1)}, u32[]{:S(2)}, u32[]{:S(2)}) collective-permute-start(bf16[128,768]{1,0:T(8,128)(2,1)S(1)} %copy-done.3), channel_id=1, source_target_pairs={{0,16},{16,0},{1,17},{17,1},{2,18},{18,2},{3,19},{19,3},{4,20},{20... | collective-permute-start | bytes 589832 | tf_op jit(solution)/shard_map/ppermute | solution.py:346
  39.2 0.1 pad_add_fusion.where_ref
  39.3 0.8 collective-permute-done.3
  40.1 4.0 %collective-permute-done = bf16[128,768]{1,0:T(8,128)(2,1)S(1)} collective-permute-done((bf16[128,768]{1,0:T(8,128)(2,1)S(1)}, bf16[128,768]{1,0:T(8,128)(2,1)S(1)}, u32[]{:S(2)}, u32[]{:S(2)}) %collective-permute-start) | collective-permute-done | bytes 196640 | tf_op jit(solution)/shard_map/ppermute | solution.py:346
  44.2 0.3 split.1
  44.5 1.9 %collective-permute-start.4 = (bf16[128,768]{1,0:T(8,128)(2,1)S(1)}, bf16[128,768]{1,0:T(8,128)(2,1)S(1)}, u32[]{:S(2)}, u32[]{:S(2)}) collective-permute-start(bf16[128,768]{1,0:T(8,128)(2,1)S(1)} %get-tuple-element.17), channel_id=1, source_target_pairs={{0,16},{16,0},{1,17},{17,1},{2,18},{18,2},{3,19},{19,3},{4,20},{20... | collective-permute-start | bytes 589832 | tf_op jit(solution)/shard_map/ppermute | solution.py:346
  46.4 5.0 %all_gather.12.near_ref.near_rows_ref = bf16[512,768]{1,0:T(8,128)(2,1)S(1)} all-gather(bf16[256,768]{1,0:T(8,128)(2,1)S(1)} %pad_maximum_fusion), channel_id=1, replica_groups=mesh['yh'=2,'zh'=2,'zm'=4,'zl'=2,'c'=2,'dp'=8] {'c'}, dimensions={0}, use_global_device_ids=true | all-gather | bytes 1179648 | tf_op jit(solution)/shard_map/all_gather | solution.py:347
  51.5 2.9 %collective-permute-start.5 = (bf16[128,768]{1,0:T(8,128)(2,1)S(1)}, bf16[128,768]{1,0:T(8,128)(2,1)S(1)}, u32[]{:S(2)}, u32[]{:S(2)}) collective-permute-start(bf16[128,768]{1,0:T(8,128)(2,1)S(1)} %get-tuple-element.20), channel_id=1, source_target_pairs={{0,16},{16,0},{1,17},{17,1},{2,18},{18,2},{3,19},{19,3},{4,20},{20... | collective-permute-start | bytes 589832 | tf_op jit(solution)/shard_map/ppermute | solution.py:346
  54.4 0.0 copy-start
  54.4 0.0 copy-start.7
  54.4 2.8 %all_gather.13.back_ref = bf16[512,768]{1,0:T(8,128)(2,1)S(1)} all-gather(bf16[256,768]{1,0:T(8,128)(2,1)S(1)} %pad_maximum_fusion.1), channel_id=1, replica_groups=mesh['yh'=2,'zh'=2,'zm'=4,'zl'=2,'c'=2,'dp'=8] {'c'}, dimensions={0}, use_global_device_ids=true | all-gather | bytes 1179648 | tf_op jit(solution)/shard_map/all_gather | solution.py:347
  57.2 2.1 %stats.1 = f32[128,128]{1,0:T(8,128)} custom-call(s32[4,12]{1,0:T(4,128)S(1)} %copy-done.7, bf16[128,768]{1,0:T(8,128)(2,1)S(1)} %copy-done.1, bf16[128,768]{1,0:T(8,128)(2,1)S(1)} %copy-done.2, bf16[128,768]{1,0:T(8,128)(2,1)S(1)} %copy-done.3, bf16[32,768]{1,0:T(8,128)(2,1)S(1)} %copy-done.6, bf16[128,768]{1,0:T(8,128)(2,1)S(1)} %copy-done, ...), custom_call_target="tpu_custom_call" | custom-call | flops 200000000 | bytes 2000000 | tf_op jit(solution)/shard_map/stats/pallas_call | solution.py:381
  59.4 11.5 %all-to-all-start.1 = ((f32[16,8,128]{2,1,0:T(8,128)}), f32[16,8,128]{2,1,0:T(8,128)S(1)}, u32[]{:S(2)}, u32[]{:S(2)}) async-start(f32[16,8,128]{2,1,0:T(8,128)} %bitcast.4), calls=%async_computation.1 | async-start | bytes 131072 | tf_op jit(solution)/shard_map/all_to_all | solution.py:338
  70.9 3.8 %forward.1 = (bf16[128,768]{1,0:T(8,128)(2,1)}, bf16[128,768]{1,0:T(8,128)(2,1)}, f32[24,128]{1,0:T(8,128)S(1)}) custom-call(s32[4,12]{1,0:T(4,128)S(1)} %copy-done.7, bf16[128,768]{1,0:T(8,128)(2,1)S(1)} %copy-done.1, bf16[128,768]{1,0:T(8,128)(2,1)S(1)} %copy-done.2, bf16[128,768]{1,0:T(8,128)(2,1)S(1)} %copy-done.4, bf16[128,768]{1,0:T(8,128)(2,1)S(1)} %copy-done.5, ...), custom_call_target="tpu_custom_call" | custom-call | flops 1000000000 | bytes 3000000 | tf_op jit(solution)/shard_map/forward/pallas_call | solution.py:390
  74.6 2.9 %all_gather.14.back_ref = bf16[512,768]{1,0:T(8,128)(2,1)S(1)} all-gather(bf16[256,768]{1,0:T(8,128)(2,1)S(1)} %pad_maximum_fusion.2), channel_id=1, replica_groups=mesh['yh'=2,'zh'=2,'zm'=4,'zl'=2,'c'=2,'dp'=8] {'c'}, dimensions={0}, use_global_device_ids=true | all-gather | bytes 1179648 | tf_op jit(solution)/shard_map/all_gather | solution.py:347
  77.5 6.0 %all_gather.15.stat_ref = f32[512,128]{1,0:T(8,128)S(1)} all-gather(f32[128,128]{1,0:T(8,128)S(1)} %bitcast.8), channel_id=1, replica_groups=mesh['yh'=2,'zh'=2,'zm'=4,'zl'=2,'c'=2,'dp'=8] {'zl','c'}, dimensions={0}, use_global_device_ids=true | all-gather | bytes 327680 | tf_op jit(solution)/shard_map/all_gather | solution.py:342
  83.5 3.5 %backward.1 = (bf16[128,768]{1,0:T(8,128)(2,1)}, bf16[128,768]{1,0:T(8,128)(2,1)}) custom-call(s32[4,12]{1,0:T(4,128)S(1)} %copy-done.7, s32[2]{0:T(128)S(1)} %pad_add_fusion.where_ref, bf16[128,768]{1,0:T(8,128)(2,1)S(1)} %copy-done.1, bf16[128,768]{1,0:T(8,128)(2,1)S(1)} %copy-done.2, bf16[128,768]{1,0:T(8,128)(2,1)S(1)} %copy-done.4, ...), custom_call_target="tpu_custom_call" | custom-call | flops 1000000000 | bytes 3000000 | tf_op jit(solution)/shard_map/backward/pallas_call | solution.py:405
  (22 shorter events, 0.1 us)
Async XLA Ops:
  3.6 19.7 %copy-start.6 = (bf16[32,768]{1,0:T(8,128)(2,1)S(1)}, bf16[32,768]{1,0:T(8,128)(2,1)}, u32[]{:S(2)}) copy-start(bf16[32,768]{1,0:T(8,128)(2,1)} %get-tuple-element.16.mid_ref) | copy-start | bytes 147460
  3.7 32.9 %copy-start.3 = (bf16[128,768]{1,0:T(8,128)(2,1)S(1)}, bf16[128,768]{1,0:T(8,128)(2,1)}, u32[]{:S(2)}) copy-start(bf16[128,768]{1,0:T(8,128)(2,1)} %get-tuple-element.14.near_ref) | copy-start | bytes 589828
  3.7 40.5 %all-to-all-start = ((bf16[16,8,768]{2,1,0:T(8,128)(2,1)}), bf16[16,8,768]{2,1,0:T(8,128)(2,1)S(1)}, u32[]{:S(2)}, u32[]{:S(2)}) async-start(bf16[16,8,768]{2,1,0:T(8,128)(2,1)} %bitcast.6), calls=%async_computation | async-start | bytes 393216 | tf_op jit(solution)/shard_map/all_to_all | solution.py:338
  23.3 16.0 %collective-permute-start.1 = (bf16[32,768]{1,0:T(8,128)(2,1)S(1)}, bf16[32,768]{1,0:T(8,128)(2,1)S(1)}, u32[]{:S(2)}, u32[]{:S(2)}) collective-permute-start(bf16[32,768]{1,0:T(8,128)(2,1)S(1)} %copy-done.6), channel_id=1, source_target_pairs={{0,64},{32,96},{64,0},{96,32},{1,65},{33,97},{65,1},{97,33},{2,66}... | collective-permute-start | bytes 147464 | tf_op jit(solution)/shard_map/ppermute | solution.py:351
  27.3 12.0 %collective-permute-start.2 = (bf16[32,768]{1,0:T(8,128)(2,1)S(1)}, bf16[32,768]{1,0:T(8,128)(2,1)S(1)}, u32[]{:S(2)}, u32[]{:S(2)}) collective-permute-start(bf16[32,768]{1,0:T(8,128)(2,1)S(1)} %copy-done.6), channel_id=1, source_target_pairs={{0,32},{32,0},{64,96},{96,64},{1,33},{33,1},{65,97},{97,65},{2,34}... | collective-permute-start | bytes 147464 | tf_op jit(solution)/shard_map/ppermute | solution.py:351
  29.5 10.6 %collective-permute-start.3 = (bf16[32,768]{1,0:T(8,128)(2,1)S(1)}, bf16[32,768]{1,0:T(8,128)(2,1)S(1)}, u32[]{:S(2)}, u32[]{:S(2)}) collective-permute-start(bf16[32,768]{1,0:T(8,128)(2,1)S(1)} %copy-done.6), channel_id=1, source_target_pairs={{0,96},{32,64},{64,32},{96,0},{1,97},{33,65},{65,33},{97,1},{2,98}... | collective-permute-start | bytes 147464 | tf_op jit(solution)/shard_map/ppermute | solution.py:351
  36.5 7.6 %collective-permute-start = (bf16[128,768]{1,0:T(8,128)(2,1)S(1)}, bf16[128,768]{1,0:T(8,128)(2,1)S(1)}, u32[]{:S(2)}, u32[]{:S(2)}) collective-permute-start(bf16[128,768]{1,0:T(8,128)(2,1)S(1)} %copy-done.3), channel_id=1, source_target_pairs={{0,16},{16,0},{1,17},{17,1},{2,18},{18,2},{3,19},{19,3},{4,20},{20... | collective-permute-start | bytes 589832 | tf_op jit(solution)/shard_map/ppermute | solution.py:346
  40.1 4.1 %copy-start.4 = (bf16[128,768]{1,0:T(8,128)(2,1)S(1)}, bf16[128,768]{1,0:T(8,128)(2,1)}, u32[]{:S(2)}) copy-start(bf16[128,768]{1,0:T(8,128)(2,1)} %q_ref.5) | copy-start | bytes 589828
  40.1 4.1 %copy-start.5 = (bf16[128,768]{1,0:T(8,128)(2,1)S(1)}, bf16[128,768]{1,0:T(8,128)(2,1)}, u32[]{:S(2)}) copy-start(bf16[128,768]{1,0:T(8,128)(2,1)} %g_ref.5) | copy-start | bytes 589828
  44.5 9.9 %collective-permute-start.4 = (bf16[128,768]{1,0:T(8,128)(2,1)S(1)}, bf16[128,768]{1,0:T(8,128)(2,1)S(1)}, u32[]{:S(2)}, u32[]{:S(2)}) collective-permute-start(bf16[128,768]{1,0:T(8,128)(2,1)S(1)} %get-tuple-element.17), channel_id=1, source_target_pairs={{0,16},{16,0},{1,17},{17,1},{2,18},{18,2},{3,19},{19,3},{4,20},{20... | collective-permute-start | bytes 589832 | tf_op jit(solution)/shard_map/ppermute | solution.py:346
  51.5 19.4 %collective-permute-start.5 = (bf16[128,768]{1,0:T(8,128)(2,1)S(1)}, bf16[128,768]{1,0:T(8,128)(2,1)S(1)}, u32[]{:S(2)}, u32[]{:S(2)}) collective-permute-start(bf16[128,768]{1,0:T(8,128)(2,1)S(1)} %get-tuple-element.20), channel_id=1, source_target_pairs={{0,16},{16,0},{1,17},{17,1},{2,18},{18,2},{3,19},{19,3},{4,20},{20... | collective-permute-start | bytes 589832 | tf_op jit(solution)/shard_map/ppermute | solution.py:346
  54.4 2.8 %copy-start = (bf16[128,768]{1,0:T(8,128)(2,1)S(1)}, bf16[128,768]{1,0:T(8,128)(2,1)}, u32[]{:S(2)}) copy-start(bf16[128,768]{1,0:T(8,128)(2,1)} %get-tuple-element.15.far_ref) | copy-start | bytes 589828
  54.4 2.8 %copy-start.1 = (bf16[128,768]{1,0:T(8,128)(2,1)S(1)}, bf16[128,768]{1,0:T(8,128)(2,1)}, u32[]{:S(2)}) copy-start(bf16[128,768]{1,0:T(8,128)(2,1)} %k_ref.5) | copy-start | bytes 589828
  54.4 2.8 %copy-start.2 = (bf16[128,768]{1,0:T(8,128)(2,1)S(1)}, bf16[128,768]{1,0:T(8,128)(2,1)}, u32[]{:S(2)}) copy-start(bf16[128,768]{1,0:T(8,128)(2,1)} %v_ref.5) | copy-start | bytes 589828
  54.4 2.8 %copy-start.7 = (s32[4,12]{1,0:T(4,128)S(1)}, s32[4,12]{1,0:T(4,128)}, u32[]{:S(2)}) copy-start(s32[4,12]{1,0:T(4,128)} %off_ref.7) | copy-start | bytes 580
  59.4 18.2 %all-to-all-start.1 = ((f32[16,8,128]{2,1,0:T(8,128)}), f32[16,8,128]{2,1,0:T(8,128)S(1)}, u32[]{:S(2)}, u32[]{:S(2)}) async-start(f32[16,8,128]{2,1,0:T(8,128)} %bitcast.4), calls=%async_computation.1 | async-start | bytes 131072 | tf_op jit(solution)/shard_map/all_to_all | solution.py:338
